TPU v7x, 32 devices: a whole 2x2x4 slice. The times are simulated.
32 devices in a mesh: wide: 16 (over z, y, x), tensor: 2 (over core).
Axes of the slice: x: 2, y: 2, z: 4, core: 2. Of those that a mesh axis runs over, the one named last changes fastest.
Arguments:
- inputs: bfloat16 [50176, 512], P(('wide', 'tensor')), may hold values from -6 to 6
- cotangent: bfloat16 [50176, 512], P(('wide', 'tensor')), may hold values from -6 to 6
- window_order: int32 [128, 392], P('wide'), may hold values from 0 to 391, as said below
- region_ids: int32 [50176], P('wide'), may hold values from 0 to 7, as said below
- clip_threshold: float32 [], replicated, may hold values from 4 to 9
- norm1_gain: bfloat16 [512], replicated, may hold values from 0.25 to 1.75
- norm1_shift: bfloat16 [512], replicated, may hold values from -1.5 to 1.5
- qkv_weight: bfloat16 [512, 1536], P('wide', 'tensor'), may hold values from -1 to 1
- qv_bias: bfloat16 [2, 512], P(None, 'tensor'), may hold values from -2.5 to 2.5
- rel_table: bfloat16 [16, 2535], P('tensor'), may hold values from -3.5 to 3.5
- out_weight: bfloat16 [512, 512], P('tensor', 'wide'), may hold values from -1 to 1
- out_bias: bfloat16 [512], replicated, may hold values from -2.5 to 2.5
- norm2_gain: bfloat16 [512], replicated, may hold values from 0.25 to 1.75
- norm2_shift: bfloat16 [512], replicated, may hold values from -1.5 to 1.5
- expand_weight: bfloat16 [512, 2048], P('wide', 'tensor'), may hold values from -0.25 to 0.25
- expand_bias: bfloat16 [2048], P('tensor'), may hold values from -2.5 to 2.5
- reduce_weight: bfloat16 [2048, 512], P('tensor', 'wide'), may hold values from -0.125 to 0.125
- reduce_bias: bfloat16 [512], replicated, may hold values from -2.5 to 2.5
Outputs:
- layer_out: bfloat16 [50176, 512], P(('wide', 'tensor'))
- input_grad: bfloat16 [50176, 512], P(('wide', 'tensor'))
- norm1_gain_grad: float32 [512], replicated
- norm1_shift_grad: float32 [512], replicated
- qkv_weight_grad: float32 [512, 1536], P('wide', 'tensor')
- qv_bias_grad: float32 [2, 512], P(None, 'tensor')
- rel_table_grad: float32 [16, 2535], P('tensor')
- out_weight_grad: float32 [512, 512], P('tensor', 'wide')
- out_bias_grad: float32 [512], replicated
- norm2_gain_grad: float32 [512], replicated
- norm2_shift_grad: float32 [512], replicated
- expand_weight_grad: float32 [512, 2048], P('wide', 'tensor')
- expand_bias_grad: float32 [2048], P('tensor')
- reduce_weight_grad: float32 [2048, 512], P('tensor', 'wide')
- reduce_bias_grad: float32 [512], replicated
- head_maxima: float32 [16], P('tensor')
- clipped_qkv: float32 [512, 1536], P('wide', 'tensor')
- clipped_bias: float32 [2, 512], P(None, 'tensor')
Inputs may be any that keep to these rules, and one draw needn't show every extreme that they name: `window_order`: each row is a permutation of the 392 positions of a window, counted frame by frame, row by row. `region_ids`: tokens of one window with equal ids lie in the same region of the shifted partition.
All inputs are finite; a program needn't handle non-finite values.
Results may differ from a plain program's by a relative error of at most 0.012.
The roundings to bfloat16 on the way count: a program that leaves them out, or rounds other values in their place, can miss the bound.
Values may be sent and summed in bfloat16 or wider, within the bound.
A program may use at most 320 MiB of HBM per device.

v0:
```python
import jax
import jax.numpy as jnp
from jax import lax
from jax.sharding import PartitionSpec as P

D = 512
HEADS = 16
HD = 32
FF = 2048
WT = 8
WH = 7
WW = 7
WIN = 392
RT = 2535


epsilon = 1e-05
masked = -100.0
lowest = -1e30


def layer_norm(rows, gain, shift):
    mean = jnp.mean(rows, axis=-1, keepdims=True)
    centered = rows - mean
    spread = jnp.mean(centered * centered, axis=-1, keepdims=True)
    return centered * lax.rsqrt(spread + epsilon) * gain + shift


def exact_gelu(values):
    return jax.nn.gelu(values, approximate=False)


def relative_index(order):
    frame_at = order // (WH * WW)
    row_at = order // WW % WH
    column_at = order % WW
    frame_off = frame_at[:, None] - frame_at[None, :] + (WT - 1)
    row_off = row_at[:, None] - row_at[None, :] + (WH - 1)
    column_off = column_at[:, None] - column_at[None, :] + (WW - 1)
    return (frame_off * (2 * WH - 1) + row_off) * (2 * WW - 1) + column_off


def inverse_order(order):
    windows = order.shape[0]
    rows_at = jnp.broadcast_to(jnp.arange(windows, dtype=jnp.int32)[:, None], order.shape)
    stored = jnp.broadcast_to(jnp.arange(WIN, dtype=jnp.int32)[None, :], order.shape)
    return jnp.zeros_like(order).at[rows_at, order].set(stored)


def reorder(rows, picks):
    return jnp.take_along_axis(rows, picks[:, :, None], axis=1)


def to_heads(canon, windows, heads):
    split = canon.reshape(windows, WIN, heads, 3, HD).transpose(0, 3, 2, 1, 4)
    return (split[:, 0], split[:, 1], split[:, 2])


def window_scores(query_win, key_win, region_win, bias):
    raw = jnp.einsum(
        "hqd,hkd->hqk", query_win, key_win, preferred_element_type=jnp.float32
    ) * HD ** (-0.5)
    same = region_win[:, None] == region_win[None, :]
    return (raw, raw + bias + jnp.where(same, 0.0, masked)[None])


def attend(queries, key_items, value_items, regions, bias):

    def one_window(item):
        query_win, key_win, value_win, region_win = item
        raw, scores = window_scores(query_win, key_win, region_win, bias)
        top = jnp.max(scores, axis=-1, keepdims=True)
        weights = jnp.exp(scores - top)
        total = jnp.sum(weights, axis=-1, keepdims=True)
        probs_low = (weights / total).astype(jnp.bfloat16)
        output = jnp.einsum(
            "hqk,hkd->hqd", probs_low, value_win, preferred_element_type=jnp.float32
        )
        return (
            output.astype(jnp.bfloat16),
            (top + jnp.log(total))[..., 0],
            jnp.max(raw, axis=(1, 2)),
        )

    return lax.map(one_window, (queries, key_items, value_items, regions))


def attend_back(queries, key_items, value_items, grad_items, log_total, regions, bias):

    def one_window(table_sum, item):
        query_win, key_win, value_win, grad_win, total_win, region_win = item
        raw, scores = window_scores(query_win, key_win, region_win, bias)
        probs = jnp.exp(scores - total_win[..., None])
        probs_low = probs.astype(jnp.bfloat16)
        value_grad = jnp.einsum(
            "hqk,hqd->hkd", probs_low, grad_win, preferred_element_type=jnp.float32
        )
        prob_grad = jnp.einsum(
            "hqd,hkd->hqk", grad_win, value_win, preferred_element_type=jnp.float32
        )
        inner = jnp.sum(probs * prob_grad, axis=-1, keepdims=True)
        score_grad = (probs * (prob_grad - inner)).astype(jnp.bfloat16)
        query_grad = jnp.einsum(
            "hqk,hkd->hqd", score_grad, key_win, preferred_element_type=jnp.float32
        ) * HD ** (-0.5)
        key_grad = jnp.einsum(
            "hqk,hqd->hkd", score_grad, query_win, preferred_element_type=jnp.float32
        ) * HD ** (-0.5)
        table_sum = table_sum + score_grad.astype(jnp.float32)
        return (
            table_sum,
            (
                query_grad.astype(jnp.bfloat16),
                key_grad.astype(jnp.bfloat16),
                value_grad.astype(jnp.bfloat16),
            ),
        )

    start = jnp.zeros(bias.shape, jnp.float32)
    table_sum, grads = lax.scan(
        one_window, start, (queries, key_items, value_items, grad_items, log_total, regions)
    )
    return (grads[0], grads[1], grads[2], table_sum)


def body(
    inputs,
    cotangent,
    window_order,
    region_ids,
    clip_threshold,
    norm1_gain,
    norm1_shift,
    qkv_weight,
    qv_bias,
    rel_table,
    out_weight,
    out_bias,
    norm2_gain,
    norm2_shift,
    expand_weight,
    expand_bias,
    reduce_weight,
    reduce_bias,
):
    parts = lax.axis_size("tensor")
    mine = lax.axis_index("tensor")
    qkv_use, out_use, expand_use, reduce_use = (
        lax.all_gather(qkv_weight, "wide", axis=0, tiled=True),
        lax.all_gather(out_weight, "wide", axis=1, tiled=True),
        lax.all_gather(expand_weight, "wide", axis=0, tiled=True),
        lax.all_gather(reduce_weight, "wide", axis=1, tiled=True),
    )
    table_use, bias_use, expand_shift = (rel_table, qv_bias, expand_bias)
    order_use, region_use = (window_order, region_ids)
    heads = table_use.shape[0]
    windows = order_use.shape[0]
    own_heads = HEADS // parts
    gain1 = norm1_gain.astype(jnp.float32)
    shift1 = norm1_shift.astype(jnp.float32)
    gain2 = norm2_gain.astype(jnp.float32)
    shift2 = norm2_shift.astype(jnp.float32)
    canon_index = relative_index(jnp.arange(WIN, dtype=jnp.int32))
    bias = jnp.take(table_use.astype(jnp.float32), canon_index, axis=1)
    inverse = inverse_order(order_use)
    regions = jnp.take_along_axis(region_use.reshape(windows, WIN), inverse, axis=1)
    inputs_wide = inputs.astype(jnp.float32)
    normed = layer_norm(inputs_wide, gain1, shift1).astype(jnp.bfloat16)
    normed_all = lax.all_gather(normed, "tensor", axis=0, tiled=True)
    head_bias = (
        jnp.stack(
            [
                bias_use[0].reshape(heads, HD),
                jnp.zeros((heads, HD), jnp.bfloat16),
                bias_use[1].reshape(heads, HD),
            ],
            axis=1,
        )
        .reshape(3 * heads * HD)
        .astype(jnp.float32)
    )
    projected = (
        jnp.dot(normed_all, qkv_use, preferred_element_type=jnp.float32) + head_bias
    ).astype(jnp.bfloat16)
    canon = reorder(projected.reshape(windows, WIN, 3 * heads * HD), inverse)
    queries, key_items, value_items = to_heads(canon, windows, heads)
    output_items, log_total, peaks = attend(queries, key_items, value_items, regions, bias)
    attended_canon = output_items.transpose(0, 2, 1, 3).reshape(windows, WIN, heads * HD)
    attended = reorder(attended_canon, order_use).reshape(windows * WIN, heads * HD)
    attention = lax.psum_scatter(
        jnp.dot(attended, out_use, preferred_element_type=jnp.float32),
        "tensor",
        scatter_dimension=0,
        tiled=True,
    )
    middle = inputs_wide + attention + out_bias.astype(jnp.float32)
    normed2 = layer_norm(middle, gain2, shift2).astype(jnp.bfloat16)
    normed2_all = lax.all_gather(normed2, "tensor", axis=0, tiled=True)
    hidden = jnp.dot(
        normed2_all, expand_use, preferred_element_type=jnp.float32
    ) + expand_shift.astype(jnp.float32)
    active = exact_gelu(hidden).astype(jnp.bfloat16)
    feed = lax.psum_scatter(
        jnp.dot(active, reduce_use, preferred_element_type=jnp.float32).astype(jnp.bfloat16),
        "tensor",
        scatter_dimension=0,
        tiled=True,
    ).astype(jnp.float32)
    layer_out = (middle + feed + reduce_bias.astype(jnp.float32)).astype(jnp.bfloat16)
    grad_all = lax.all_gather(cotangent, "tensor", axis=0, tiled=True)
    reduce_grad = jnp.einsum("rf,rd->fd", active, grad_all, preferred_element_type=jnp.float32)
    active_grad = jnp.einsum("rd,fd->rf", grad_all, reduce_use, preferred_element_type=jnp.float32)
    hidden_grad = jax.vjp(exact_gelu, hidden)[1](active_grad)[0].astype(jnp.bfloat16)
    expand_grad = jnp.einsum(
        "rd,rf->df", normed2_all, hidden_grad, preferred_element_type=jnp.float32
    )
    expand_bias_grad = jnp.sum(hidden_grad.astype(jnp.float32), axis=0)
    normed2_grad = lax.psum_scatter(
        jnp.einsum("rf,df->rd", hidden_grad, expand_use, preferred_element_type=jnp.float32),
        "tensor",
        scatter_dimension=0,
        tiled=True,
    )
    middle_norm_grad, gain2_grad, shift2_grad = jax.vjp(layer_norm, middle, gain2, shift2)[1](
        normed2_grad
    )
    middle_grad = cotangent.astype(jnp.float32) + middle_norm_grad
    attention_grad = middle_grad.astype(jnp.bfloat16)
    attention_grad_all = lax.all_gather(attention_grad, "tensor", axis=0, tiled=True)
    out_grad = jnp.einsum(
        "ra,rd->ad", attended, attention_grad_all, preferred_element_type=jnp.float32
    )
    out_bias_grad = jnp.sum(attention_grad.astype(jnp.float32), axis=0)
    attended_grad = jnp.einsum(
        "rd,ad->ra", attention_grad_all, out_use, preferred_element_type=jnp.float32
    ).astype(jnp.bfloat16)
    grad_canon = reorder(attended_grad.reshape(windows, WIN, heads * HD), inverse)
    grad_items = grad_canon.reshape(windows, WIN, heads, HD).transpose(0, 2, 1, 3)
    query_grad, key_grad, value_grad, table_sum = attend_back(
        queries, key_items, value_items, grad_items, log_total, regions, bias
    )
    stacked = jnp.stack([query_grad, key_grad, value_grad], axis=2)
    projected_canon = stacked.transpose(0, 3, 1, 2, 4).reshape(windows, WIN, heads * 3 * HD)
    projected_grad = reorder(projected_canon, order_use).reshape(windows * WIN, heads * 3 * HD)
    qkv_grad = jnp.einsum(
        "rd,rc->dc", normed_all, projected_grad, preferred_element_type=jnp.float32
    )
    column_sums = jnp.sum(projected_grad.astype(jnp.float32), axis=0).reshape(heads, 3, HD)
    bias_grad = jnp.stack(
        [column_sums[:, 0].reshape(heads * HD), column_sums[:, 2].reshape(heads * HD)], axis=0
    )
    table_grad = jax.ops.segment_sum(
        table_sum.reshape(heads, WIN * WIN).T, canon_index.reshape(WIN * WIN), num_segments=RT
    ).T
    head_peak = jnp.max(peaks, axis=0)
    normed_grad = lax.psum_scatter(
        jnp.einsum("rc,dc->rd", projected_grad, qkv_use, preferred_element_type=jnp.float32),
        "tensor",
        scatter_dimension=0,
        tiled=True,
    )
    input_norm_grad, gain1_grad, shift1_grad = jax.vjp(layer_norm, inputs_wide, gain1, shift1)[1](
        normed_grad
    )
    input_grad = (middle_grad + input_norm_grad).astype(jnp.bfloat16)
    reduce_bias_grad = jnp.sum(cotangent.astype(jnp.float32), axis=0)
    offset = mine * heads
    table_full = lax.dynamic_update_slice(
        jnp.zeros((HEADS, RT), jnp.float32), table_grad, (offset, 0)
    )
    bias_full = lax.dynamic_update_slice(
        jnp.zeros((2, D), jnp.float32), bias_grad, (0, offset * HD)
    )
    expand_bias_full = lax.dynamic_update_slice(
        jnp.zeros((FF,), jnp.float32), expand_bias_grad, (mine * expand_bias_grad.shape[0],)
    )
    peak_full = lax.dynamic_update_slice(
        jnp.full((HEADS,), lowest, jnp.float32), head_peak, (offset,)
    )
    qkv_out, out_out, expand_out, reduce_out = (
        lax.psum_scatter(qkv_grad, "wide", scatter_dimension=0, tiled=True),
        lax.psum_scatter(out_grad, "wide", scatter_dimension=1, tiled=True),
        lax.psum_scatter(expand_grad, "wide", scatter_dimension=0, tiled=True),
        lax.psum_scatter(reduce_grad, "wide", scatter_dimension=1, tiled=True),
    )
    sums = lax.psum(
        (
            gain1_grad,
            shift1_grad,
            bias_full,
            table_full,
            out_bias_grad,
            gain2_grad,
            shift2_grad,
            expand_bias_full,
            reduce_bias_grad,
        ),
        ("wide", "tensor"),
    )
    peak_all = lax.pmax(peak_full, ("wide", "tensor"))
    head_start = mine * own_heads
    bias_own = lax.dynamic_slice_in_dim(sums[2], head_start * HD, own_heads * HD, 1)
    table_own = lax.dynamic_slice_in_dim(sums[3], head_start, own_heads, 0)
    expand_bias_own = lax.dynamic_slice_in_dim(sums[7], mine * (FF // parts), FF // parts, 0)
    peak_own = lax.dynamic_slice_in_dim(peak_all, head_start, own_heads, 0)
    factor = jnp.sqrt(clip_threshold / jnp.maximum(peak_own, clip_threshold))
    column_factor = jnp.stack([factor, factor, jnp.ones_like(factor)], axis=1)
    clipped_qkv = (
        qkv_weight.astype(jnp.float32).reshape(qkv_weight.shape[0], own_heads, 3, HD)
        * column_factor[None, :, :, None]
    ).reshape(qkv_weight.shape)
    bias_scale = jnp.stack(
        [jnp.repeat(factor, HD), jnp.ones((own_heads * HD,), jnp.float32)], axis=0
    )
    clipped_bias = qv_bias.astype(jnp.float32) * bias_scale
    return (
        layer_out,
        input_grad,
        sums[0],
        sums[1],
        qkv_out,
        bias_own,
        table_own,
        out_out,
        sums[4],
        sums[5],
        sums[6],
        expand_out,
        expand_bias_own,
        reduce_out,
        sums[8],
        peak_own,
        clipped_qkv,
        clipped_bias,
    )


def solution(mesh):
    in_specs = (
        P(("wide", "tensor"), None),
        P(("wide", "tensor"), None),
        P("wide", None),
        P("wide"),
        P(),
        P(),
        P(),
        P("wide", "tensor"),
        P(None, "tensor"),
        P("tensor", None),
        P("tensor", "wide"),
        P(),
        P(),
        P(),
        P("wide", "tensor"),
        P("tensor"),
        P("tensor", "wide"),
        P(),
    )
    out_specs = (
        P(("wide", "tensor"), None),
        P(("wide", "tensor"), None),
        P(),
        P(),
        P("wide", "tensor"),
        P(None, "tensor"),
        P("tensor", None),
        P("tensor", "wide"),
        P(),
        P(),
        P(),
        P("wide", "tensor"),
        P("tensor"),
        P("tensor", "wide"),
        P(),
        P("tensor"),
        P("wide", "tensor"),
        P(None, "tensor"),
    )
    return jax.shard_map(body, mesh=mesh, in_specs=in_specs, out_specs=out_specs, check_vma=False)
```

profile of v0, /device:TPU:0, one launch (start us, length us, event | category | flops | bytes accessed | tf_op | source)
XLA Modules:
  0.0 2580.6 jit_solution(10750587832331992622)
XLA Ops:
  15.9 15.8 scatter_custom_fusion.1
  32.7 281.5 %gather_fusion = f32[153664,8]{1,0:T(8,128)} fusion(f32[8,2535]{0,1:T(8,128)S(1)} %copy.55, s32[154624]{0:T(1024)S(1)} %pad_clamp_fusion), kind=kCustom, calls=%fused_computation.4 | custom fusion | bytes 10449152 | tf_op jit(solution)/shard_map/jit(_take)/gather | solution.py:164
  314.2 52.7 %copy.56 = f32[392,392,8]{0,1,2:T(8,128)} copy(f32[392,392,8]{2,1,0:T(8,128)} %bitcast.18) | data formatting | bytes 9834496 | tf_op jit(solution)/shard_map/jit(_take)/gather | solution.py:164
  368.1 18.5 gather_fusion.1
  386.8 43.9 %all_gather.26 = bf16[256,512]{0,1:T(8,128)(2,1)S(1)} all-gather(bf16[256,32]{0,1:T(8,128)(2,1)S(1)} %copy-done.52), channel_id=1, replica_groups=mesh['wide'=16,'tensor'=2] {'wide'}, dimensions={1}, use_global_device_ids=true | all-gather | bytes 278528 | tf_op jit(solution)/shard_map/all_gather | solution.py:150
  430.8 40.1 %all_gather.25 = bf16[512,768]{1,0:T(8,128)(2,1)S(1)} all-gather(bf16[32,768]{1,0:T(8,128)(2,1)S(1)} %copy-done.27), channel_id=1, replica_groups=mesh['wide'=16,'tensor'=2] {'wide'}, dimensions={0}, use_global_device_ids=true | all-gather | bytes 835584 | tf_op jit(solution)/shard_map/all_gather | solution.py:149
  470.9 6.9 select_bitcast_fusion
  477.9 6.8 add_convert_fusion.1
  484.6 53.5 %gather_fusion.2 = bf16[3136,768]{1,0:T(8,128)(2,1)} fusion(bf16[8,392,768]{2,1,0:T(8,128)(2,1)} %bitcast.187, s32[3136]{0:T(1024)S(1)} %reshape.720), kind=kCustom, calls=%fused_computation.clone | custom fusion | bytes 9658880 | tf_op jit(solution)/shard_map/jit(take_along_axis)/gather | solution.py:51
  538.1 8.0 copy.53
  553.9 82.2 %while.31 = (s32[]{:T(128)}, bf16[8,8,392,32]{2,3,1,0:T(8,128)(2,1)}, f32[8,8,392]{2,1,0:T(8,128)}, f32[8,8]{1,0:T(8,128)}, bf16[8,8,392,32]{2,3,1,0:T(8,128)(2,...) while((s32[]{:T(128)}, ...), condition=%wide.region_7.9_spmd, body=%wide.region_3.8_spmd.sunk | while | flops 170049600 | bytes 23751988 | solution.py:85
  640.5 28.5 %gather_fusion.3 = bf16[3136,256]{1,0:T(8,128)(2,1)S(1)} fusion(bf16[8,392,256]{2,1,0:T(8,128)(2,1)S(1)} %copy.57, s32[3136]{0:T(1024)S(1)} %reshape.724), kind=kCustom, calls=%fused_computation.1.clone | custom fusion | bytes 3236352 | tf_op jit(solution)/shard_map/jit(take_along_axis)/gather | solution.py:51
  675.2 12.2 reduce-scatter.9.cloned.1.call-done
  694.7 36.5 %all-gather.11.cloned.1.call-done = bf16[512,1024]{1,0:T(8,128)(2,1)} async-done(((bf16[32,1024]{1,0:T(8,128)(2,1)}), bf16[512,1024]{1,0:T(8,128)(2,1)}) %all-gather.11.cloned.1.call-update) | async-done | bytes 1048592 | tf_op jit(solution)/shard_map/all_gather | solution.py:151
  731.2 13.0 all-gather.9.cloned.1.call-done
  744.3 33.6 %multiply_convert_fusion.1 = (bf16[3136,1024]{1,0:T(8,128)(2,1)}, f32[3136,1024]{1,0:T(8,128)}, f32[3136,1024]{1,0:T(8,128)}) fusion(f32[1024]{0:T(1024)S(1)} %convert_element_type.126, bf16[3136,512]{1,0:T(8,128)(2,1)} %all-gather.9.cloned.1.call-done, bf16[512,1024]{1,0:T(8,128)(2,1)} %all-gather.11.cloned.1.call-done), kind=kOutput, calls=%fused_computation.73 | convolution fusion | flops 3500277760 | bytes 36376576 | tf_op jit(solution)/shard_map/dot_general | solution.py:199
  777.9 26.0 %all-gather.13.cloned.1.call-done = bf16[1024,512]{0,1:T(8,128)(2,1)} async-done(((bf16[1024,32]{0,1:T(8,128)(2,1)}), bf16[1024,512]{0,1:T(8,128)(2,1)}) %all-gather.13.cloned.1.call-update) | async-done | bytes 1048592 | tf_op jit(solution)/shard_map/all_gather | solution.py:152
  803.9 12.6 all-gather.15.cloned.1.call-done
  816.5 15.8 convert_reduce_fusion
  840.7 8.4 convolution_convert_fusion
  849.8 6.5 reduce-scatter.13.cloned.1.call-done
  859.9 10.8 reduce-scatter.11.cloned.1.call-done
  880.2 11.6 all-gather.17.cloned.1.call-done
  894.7 28.9 %gather_fusion.4 = bf16[3136,256]{1,0:T(8,128)(2,1)S(1)} fusion(bf16[8,392,256]{2,1,0:T(8,128)(2,1)S(1)} %bitcast.188, s32[3136]{0:T(1024)S(1)} %copy-done.5), kind=kCustom, calls=%fused_computation.3.clone | custom fusion | bytes 3236352 | tf_op jit(solution)/shard_map/jit(take_along_axis)/gather | solution.py:51
  932.6 257.5 %while.32 = (s32[]{:T(128)}, f32[8,392,392]{1,2,0:T(8,128)}, bf16[8,8,392,32]{2,3,1,0:T(8,128)(2,1)}, bf16[8,8,392,32]{2,3,1,0:T(8,128)(2,1)}, bf16[8,8,392,32]{...) while((s32[]{:T(128)}, f32[8,392,392]{1,2,0:T(8,128)}, ...), condition=%wide.region_17.20_spmd.clone, body=%wide.region_15.19_spmd.clone.sunk | while | flops 410166848 | bytes 109242976 | solution.py:120
  943.5 10.0 select_add_fusion.2
  974.1 11.8 select_add_fusion.2
  1006.5 11.8 select_add_fusion.2
  1038.9 11.8 select_add_fusion.2
  1071.3 11.8 select_add_fusion.2
  1103.7 11.8 select_add_fusion.2
  1136.2 11.8 select_add_fusion.2
  1168.6 11.8 select_add_fusion.2
  1190.1 8.2 copy.61
  1198.3 8.5 reshape.651
  1206.8 35.0 %copy.62 = f32[153664,8]{1,0:T(8,128)} copy(f32[153664,8]{0,1:T(8,128)} %bitcast.191) | data formatting | bytes 9834496 | tf_op jit(solution)/shard_map/transpose | solution.py:253
  1241.8 819.4 %scatter_custom_fusion = f32[2535,8]{1,0:T(8,128)S(1)} fusion(s32[153664]{0:T(1024)} %reshape.701, f32[153664,8]{1,0:T(8,128)} %copy.62, f32[]{:T(128)} %constant.101.clone.1), kind=kCustom, calls=%fused_computation.131 | custom fusion | flops 1229312 | bytes 81632 | tf_op jit(solution)/shard_map/scatter-add | solution.py:252
  2068.9 8.2 copy.60
  2077.1 56.4 %gather_fusion.5 = bf16[3136,768]{1,0:T(8,128)(2,1)} fusion(bf16[8,392,768]{2,1,0:T(8,128)(2,1)} %copy.60, s32[3136]{0:T(1024)S(1)} %copy-done.3), kind=kCustom, calls=%fused_computation.2.clone | custom fusion | bytes 9658880 | tf_op jit(solution)/shard_map/jit(take_along_axis)/gather | solution.py:51
  2143.7 8.9 fusion.97
  2152.8 8.9 fusion.98
  2167.2 40.5 %pmax.7 = f32[16]{0:T(128)S(1)} all-reduce(f32[16]{0:T(128)S(1)} %dynamic_update_slice.36), channel_id=1, replica_groups=mesh['wide'=16,'tensor'=2] {'wide','tensor'}, use_global_device_ids=true, to_apply=%region_44.47 | all-reduce | flops 16 | bytes 128 | tf_op jit(solution)/shard_map/pmax | solution.py:300
  2208.3 7.5 fusion.95
  2228.0 42.1 %all-reduce.1 = (f32[512]{0:T(512)}, f32[512]{0:T(512)}, f32[2,512]{1,0:T(2,128)S(1)}, f32[512]{0:T(512)}, f32[512]{0:T(512)}, /*index=5*/f32[512]{0:T(512)}, f32[2048]{0:T(1024)S(1)}, f32[512]{0:T(512)}) all-reduce(f32[512]{0:T(512)S(1)} %get-tuple-element.182, ...), channel_id=1, replica_groups=mesh['wide'=16,'tensor'=2] {'wide','tensor'}, use_global_device_ids=true, to_apply=%region_22.25 | all-reduce | flops 6144 | bytes 49152 | tf_op jit(solution)/shard_map/psum | solution.py:286
  2271.2 17.8 reduce-scatter.21.cloned.1.call-done
  2289.0 80.2 %reduce-scatter.23.cloned.1.call-done = f32[1024,32]{0,1:T(8,128)} async-done(((f32[1024,512]{0,1:T(8,128)}), f32[1024,32]{0,1:T(8,128)}) %reduce-scatter.23.cloned.1.call-update) | async-done | bytes 131088 | tf_op jit(solution)/shard_map/reduce_scatter | solution.py:284
  2369.3 76.8 %reduce-scatter.19.cloned.1.call-done = f32[256,32]{0,1:T(8,128)} async-done(((f32[256,512]{0,1:T(8,128)}), f32[256,32]{0,1:T(8,128)}) %reduce-scatter.19.cloned.1.call-update) | async-done | bytes 32784 | tf_op jit(solution)/shard_map/reduce_scatter | solution.py:282
  2446.0 127.0 %reduce-scatter.17.cloned.1.call-done = f32[32,768]{1,0:T(8,128)} async-done(((f32[512,768]{1,0:T(8,128)}), f32[32,768]{1,0:T(8,128)}) %reduce-scatter.17.cloned.1.call-update) | async-done | bytes 98320 | tf_op jit(solution)/shard_map/reduce_scatter | solution.py:281
  (465 shorter events, 353.0 us)
Async XLA Ops:
  8.1 469.8 %all-gather.7.cloned.1.call-start = ((), (), s32[]{:S(2)}) async-start(), calls=%async_computation.8 | async-start | bytes 4816896 | tf_op jit(solution)/shard_map/all_gather | solution.py:169
  14.0 17.9 copy-start.54
  14.0 18.4 copy-start.47
  14.0 673.4 %reduce-scatter.9.cloned.1.call-start = ((), (), s32[]{:S(2)}) async-start(), calls=%async_computation.9 | async-start | bytes 9633792 | tf_op jit(solution)/shard_map/reduce_scatter | solution.py:190
  14.1 352.8 %copy-start.32 = (s32[392]{0:T(512)}, s32[392]{0:T(512)S(1)}, u32[]{:S(2)}) copy-start(s32[392]{0:T(512)S(1)} %get-tuple-element.269) | copy-start | bytes 4708
  14.1 352.8 %copy-start.34 = (s32[392]{0:T(512)}, s32[392]{0:T(512)S(1)}, u32[]{:S(2)}) copy-start(s32[392]{0:T(512)S(1)} %get-tuple-element.270) | copy-start | bytes 4708
  14.2 352.7 %copy-start.36 = (s32[392]{0:T(512)}, s32[392]{0:T(512)S(1)}, u32[]{:S(2)}) copy-start(s32[392]{0:T(512)S(1)} %add_select_fusion.3) | copy-start | bytes 4708
  32.5 452.2 %copy-start.4 = (s32[3136]{0:T(1024)}, s32[3136]{0:T(1024)S(1)}, u32[]{:S(2)}) copy-start(s32[3136]{0:T(1024)S(1)} %reshape.720) | copy-start | bytes 37636
  314.2 53.7 %copy-start.53 = (s32[3136]{0:T(1024)S(1)}, s32[3136]{0:T(1024)}, u32[]{:S(2)}) copy-start(s32[3136]{0:T(1024)} %param.29) | copy-start | bytes 37636
  368.0 18.8 copy-start.52
  368.0 62.8 %copy-start.27 = (bf16[32,768]{1,0:T(8,128)(2,1)S(1)}, bf16[32,768]{1,0:T(8,128)(2,1)}, u32[]{:S(2)}) copy-start(bf16[32,768]{1,0:T(8,128)(2,1)} %param.33) | copy-start | bytes 147460
  386.8 253.7 %copy-start.2 = (s32[3136]{0:T(1024)}, s32[3136]{0:T(1024)S(1)}, u32[]{:S(2)}) copy-start(s32[3136]{0:T(1024)S(1)} %reshape.724) | copy-start | bytes 37636
  430.8 238.9 %copy-start.20 = (bf16[256,512]{0,1:T(8,128)(2,1)}, bf16[256,512]{0,1:T(8,128)(2,1)S(1)}, u32[]{:S(2)}) copy-start(bf16[256,512]{0,1:T(8,128)(2,1)S(1)} %all_gather.26) | copy-start | bytes 786436
  430.8 115.3 %copy-start.50 = (pred[8,392]{1,0:T(8,128)(4,1)}, pred[8,392]{1,0:T(8,128)(4,1)S(1)}, u32[]{:S(2)}) copy-start(pred[8,392]{1,0:T(8,128)(4,1)S(1)} %and_bitcast_fusion.1) | copy-start | bytes 9412
  430.8 238.2 %copy-start.48 = (pred[8,392]{1,0:T(8,128)(4,1)}, pred[8,392]{1,0:T(8,128)(4,1)S(1)}, u32[]{:S(2)}) copy-start(pred[8,392]{1,0:T(8,128)(4,1)S(1)} %and_bitcast_fusion) | copy-start | bytes 9412
  674.5 56.7 %all-gather.11.cloned.1.call-start = ((), (), s32[]{:S(2)}) async-start(), calls=%async_computation.11 | async-start | bytes 1114112 | tf_op jit(solution)/shard_map/all_gather | solution.py:151
  675.1 69.2 %all-gather.9.cloned.1.call-start = ((), (), s32[]{:S(2)}) async-start(), calls=%async_computation.10 | async-start | bytes 4816896 | tf_op jit(solution)/shard_map/all_gather | solution.py:198
  693.3 110.6 %all-gather.13.cloned.1.call-start = ((), (), s32[]{:S(2)}) async-start(), calls=%async_computation.12 | async-start | bytes 1114112 | tf_op jit(solution)/shard_map/all_gather | solution.py:152
  693.9 122.6 %all-gather.15.cloned.1.call-start = ((), (), s32[]{:S(2)}) async-start(), calls=%async_computation.14 | async-start | bytes 4816896 | tf_op jit(solution)/shard_map/all_gather | solution.py:210
  694.6 161.6 %reduce-scatter.13.cloned.1.call-start = ((), (), s32[]{:S(2)}) async-start(), calls=%async_computation.15 | async-start | bytes 9633792 | tf_op jit(solution)/shard_map/reduce_scatter | solution.py:218
  816.5 18.4 copy-start.70
  840.5 30.2 %reduce-scatter.11.cloned.1.call-start = ((), (), s32[]{:S(2)}) async-start(), calls=%async_computation.13 | async-start | bytes 4816896 | tf_op jit(solution)/shard_map/reduce_scatter | solution.py:203
  849.1 42.7 %all-gather.17.cloned.1.call-start = ((), (), s32[]{:S(2)}) async-start(), calls=%async_computation.16 | async-start | bytes 4816896 | tf_op jit(solution)/shard_map/all_gather | solution.py:229
  849.8 10.1 copy-start.42
  878.1 13.7 copy-start.21
  878.2 1339.9 %all-reduce.4.cloned.1.call-start = ((), (), s32[]{:S(2)}) async-start(), calls=%async_computation.19 | async-start | bytes 327680 | tf_op jit(solution)/shard_map/psum | solution.py:286
  880.2 14.5 copy-start.5
  894.7 28.9 %copy-start.51 = (pred[8,392]{1,0:T(8,128)(4,1)S(1)}, pred[8,392]{1,0:T(8,128)(4,1)}, u32[]{:S(2)}) copy-start(pred[8,392]{1,0:T(8,128)(4,1)} %copy-done.50) | copy-start | bytes 9412
  935.0 8.6 copy-start
  997.9 8.6 copy-start
  1030.3 8.6 copy-start
  1062.7 8.6 copy-start
  1095.1 8.6 copy-start
  1127.6 8.6 copy-start
  1160.0 8.6 copy-start
  1241.8 820.5 %copy-start.18 = (bf16[8,8,392,32]{2,3,1,0:T(8,128)(2,1)S(1)}, bf16[8,8,392,32]{2,3,1,0:T(8,128)(2,1)}, u32[]{:S(2)}) copy-start(bf16[8,8,392,32]{2,3,1,0:T(8,128)(2,1)} %get-tuple-element.136) | copy-start | bytes 4816900
  2062.3 157.3 %reduce-scatter.15.cloned.1.call-start = ((), (), s32[]{:S(2)}) async-start(), calls=%async_computation.17 | async-start | bytes 9633792 | tf_op jit(solution)/shard_map/reduce_scatter | solution.py:256
  2077.1 56.4 %copy-start.49 = (pred[8,392]{1,0:T(8,128)(4,1)S(1)}, pred[8,392]{1,0:T(8,128)(4,1)}, u32[]{:S(2)}) copy-start(pred[8,392]{1,0:T(8,128)(4,1)} %copy-done.48) | copy-start | bytes 9412
  2143.7 145.4 %reduce-scatter.21.cloned.1.call-start = ((), (), s32[]{:S(2)}) async-start(), calls=%async_computation.21 | async-start | bytes 2228224 | tf_op jit(solution)/shard_map/reduce_scatter | solution.py:283
  2152.7 9.3 copy-start.17
  2152.7 216.6 %reduce-scatter.23.cloned.1.call-start = ((), (), s32[]{:S(2)}) async-start(), calls=%async_computation.22 | async-start | bytes 2228224 | tf_op jit(solution)/shard_map/reduce_scatter | solution.py:284
  2161.7 284.4 %reduce-scatter.19.cloned.1.call-start = ((), (), s32[]{:S(2)}) async-start(), calls=%async_computation.20 | async-start | bytes 557056 | tf_op jit(solution)/shard_map/reduce_scatter | solution.py:282
  2166.2 406.9 %reduce-scatter.17.cloned.1.call-start = ((), (), s32[]{:S(2)}) async-start(), calls=%async_computation.18 | async-start | bytes 1671168 | tf_op jit(solution)/shard_map/reduce_scatter | solution.py:281
  2208.3 8.6 copy-start.28
  2208.3 9.2 copy-start.60
  2208.3 11.3 copy-start.7
  2208.3 11.3 copy-start.26
  2208.3 11.3 copy-start.46
  (67 other events, 235.8 us)
Sparse Core Ops, SparseCore 0:
  14.2 14.9 all-gather.6
  674.6 12.7 reduce-scatter.8
  878.3 13.4 all-gather.16
  2062.4 122.9 all-reduce.3
  2187.7 16.6 reduce-scatter.14
  2207.1 81.9 reduce-scatter.20
  2291.9 77.3 reduce-scatter.22
  2372.1 73.9 reduce-scatter.18
  2452.1 120.8 reduce-scatter.16
Sparse Core Ops, SparseCore 1:
  677.7 53.4 all-gather.10
  733.3 10.9 all-gather.8
  747.3 56.5 all-gather.12
  805.5 10.9 all-gather.14
  840.6 15.6 reduce-scatter.12
  858.5 12.0 reduce-scatter.10
where the time goes:
time: 2590 us; the launch traced here: 2580 us
  other arithmetic  978 us (38%)
  local copies, waits for them, and re-layouts  671 us (26%)
  waiting for transfers between devices  433 us (17%)
  matrix products  312 us (12%)
  blocking collectives  167 us (6%)
    scatter-add x1, other arithmetic, body(): jax.ops.segment_sum(table_sum.reshape(heads, WIN * WIN).T, canon_index.re...  819 us
    gather x2, local copies, waits for them, and re-layouts, body(): bias = jnp.take(table_use.astype(jnp.float32), canon_index, axis=1)  334 us
    gather x7, local copies, waits for them, and re-layouts, reorder(): return jnp.take_along_axis(rows, picks[:, :, None], axis=1)  175 us
    reduce_scatter x1, waiting for transfers between devices, body(): lax.psum_scatter(qkv_grad, 'wide', scatter_dimension=0, tiled=True)  127 us
    add x8, other arithmetic, one_window(): table_sum = table_sum + score_grad.astype(jnp.float32)  92.5 us
    dot_general x16, matrix products, window_scores(): jnp.einsum('hqd,hkd->hqk', query_win, key_win, preferred_element_type=jnp...  83.5 us
    reduce_scatter x1, waiting for transfers between devices, body(): lax.psum_scatter(reduce_grad, 'wide', scatter_dimension=1, tiled=True)  80.2 us
    reduce_scatter x1, waiting for transfers between devices, body(): lax.psum_scatter(out_grad, 'wide', scatter_dimension=1, tiled=True)  76.8 us
  transfers between devices with their start and end apart: 15, of which 12 were waited for; matrix products, arithmetic and copies ran while one was open for 21% of the time, Pallas kernels for 0%

commit v1 on v0

v1 whole, which is shorter than its diff:
```python
import functools
import math

import jax
import jax.numpy as jnp
from jax import lax
from jax.experimental import pallas as pl
from jax.experimental.pallas import tpu as pltpu
from jax.sharding import PartitionSpec as P

D = 512
HEADS = 16
HD = 32
FF = 2048
WT = 8
WH = 7
WW = 7
SP = WH * WW
WIN = 392
RT = 2535
ROWS = 13 * 13
GRP = 4

epsilon = 1e-05
masked = -100.0
lowest = -1e30
LOG2E = 1.4426950408889634
SCALE = HD ** (-0.5)
WIDE_SEG = 13 * WW * WT
WIDE_PAD = 768
FLAT = ROWS * WT
FLAT_PAD = 1408

f32 = jnp.float32
bf16 = jnp.bfloat16
NN = (((1,), (0,)), ((), ()))
NT = (((1,), (1,)), ((), ()))

VMEM_LIMIT = 60 * 2**20


def dot(a, b, dims=NN):
    return lax.dot_general(a, b, dims, preferred_element_type=f32)


def chunks(total, size):
    starts = list(range(0, total - size + 1, size))
    sizes = [size] * len(starts)
    rest = total - size * len(starts)
    if rest:
        if rest < size // 2:
            sizes[-1] += rest
        else:
            starts.append(size * len(starts))
            sizes.append(rest)
    return list(zip(starts, sizes))


ROW_CHUNKS = chunks(WIN, 64)


def iota(shape, axis):
    return lax.broadcasted_iota(jnp.int32, shape, axis)


def head_lanes(hh):
    return (iota((1, GRP * HD), 1) // HD == hh).astype(f32).astype(bf16)


def picks_in(place_row):
    return (iota((WIN, WIN), 0) == place_row).astype(f32).astype(bf16)


def picks_out(place_column):
    return (iota((WIN, WIN), 1) == place_column).astype(f32).astype(bf16)


def moments(rows):
    mean = jnp.mean(rows, axis=-1, keepdims=True)
    centered = rows - mean
    spread = jnp.mean(centered * centered, axis=-1, keepdims=True)
    return centered, lax.rsqrt(spread + epsilon)


def one_hot_flat():
    column = iota((FLAT_PAD, WIDE_PAD), 1)
    target = column // (WW * WT) * (13 * WT) + column % (WW * WT)
    hit = (iota((FLAT_PAD, WIDE_PAD), 0) == target) & (column < WIDE_SEG)
    return hit.astype(f32).astype(bf16)


def table_kernel(flat_ref, bias_ref, wide_ref):
    spread = one_hot_flat()
    flat = flat_ref[...]
    for wi in range(WW):
        shift = (WW - 1 - wi) * WT
        moved = pltpu.roll(flat, FLAT_PAD - shift, 1) if shift else flat
        wide_ref[...] = dot(moved.astype(bf16), spread) * LOG2E
        for hi in range(WH):
            at = (hi * WW + wi) * WT
            off = (WH - 1 - hi) * WW * WT
            rows = wide_ref[:, off : off + WIN]
            bias_ref[:, at : at + WT, :] = rows.reshape(HEADS, WT, WIN)


def table_bias(table):
    parts = table.astype(f32).reshape(HEADS, 2 * WT - 1, ROWS)[:, :, ::-1]
    flat = jnp.stack([parts[:, WT - 1 - tj : 2 * WT - 1 - tj] for tj in range(WT)], axis=-1)
    flat = flat.reshape(HEADS * WT, FLAT)
    flat = jnp.pad(flat, ((0, 0), (0, FLAT_PAD - FLAT)))
    return pl.pallas_call(
        table_kernel,
        out_shape=jax.ShapeDtypeStruct((HEADS, WIN, WIN), f32),
        scratch_shapes=[pltpu.VMEM((HEADS * WT, WIDE_PAD), f32)],
        compiler_params=pltpu.CompilerParams(vmem_limit_bytes=VMEM_LIMIT),
        name="table_bias",
    )(flat)


def table_back(flat_grad):
    parts = flat_grad[:, :FLAT].reshape(HEADS, WT, ROWS, WT)
    total = jnp.zeros((HEADS, 2 * WT - 1, ROWS), f32)
    for tj in range(WT):
        low = WT - 1 - tj
        total = total + jnp.pad(parts[:, :, :, tj], ((0, 0), (low, WT - 1 - low), (0, 0)))
    return total[:, :, ::-1].reshape(HEADS, RT)


def attend_kernel(
    kr, kc, rr, rc, x_ref, w_ref, wb_ref, bias_ref, wo_ref, bo_ref, g1, s1, g2, s2,
    xc_ref, nrm_ref, qkv_ref, e_ref, linv_ref, att_ref, mid_ref, n2_ref, hm_ref,
    x_scr, mask_scr,
):
    w = pl.program_id(0)
    pick = picks_in(kr[0])
    canon = dot(pick, x_ref[...])
    xc_ref[...] = canon.astype(bf16)
    row_at = jnp.sum(jnp.where(iota((WIN, WIN), 0) == kr[0], rr[0], 0.0), axis=1, keepdims=True)
    column_at = jnp.sum(jnp.where(iota((WIN, WIN), 1) == kc[0], rc[0], 0.0), axis=0, keepdims=True)
    mask_scr[...] = jnp.where(row_at == column_at, 0.0, masked * LOG2E)
    for at, size in ROW_CHUNKS:
        rows = xc_ref[at : at + size, :].astype(f32)
        centered, rstd = moments(rows)
        nrm_ref[at : at + size, :] = (centered * rstd * g1[...] + s1[...]).astype(bf16)
    for part in range(3):
        cols = slice(part * D, (part + 1) * D)
        qkv_ref[:, cols] = (dot(nrm_ref[...], w_ref[:, cols]) + wb_ref[:, cols]).astype(bf16)

    @pl.when(w == 0)
    def _():
        hm_ref[...] = jnp.full(hm_ref.shape, lowest, f32)

    def group(g, carry):
        off = pl.multiple_of(g * (GRP * HD), GRP * HD)
        qg = qkv_ref[:, pl.ds(off, GRP * HD)]
        kg = qkv_ref[:, pl.ds(D + off, GRP * HD)]
        vg = qkv_ref[:, pl.ds(2 * D + off, GRP * HD)]
        for hh in range(GRP):
            h = g * GRP + hh
            lanes = head_lanes(hh)
            slot = x_scr.at[hh % 2]
            slot[...] = dot(qg * lanes, kg, NT)
            top = hm_ref[h]
            sums = []
            for at, size in ROW_CHUNKS:
                xx = slot[at : at + size, :]
                top = jnp.maximum(top, jnp.max(xx.reshape(size // 8, 8, WIN), axis=0))
                s = xx * (SCALE * LOG2E) + bias_ref[h, at : at + size, :] + mask_scr[at : at + size, :]
                p = jnp.exp2(s - jnp.max(s, axis=1, keepdims=True))
                sums.append(jnp.sum(p, axis=1, keepdims=True))
                e_ref[0, h, at : at + size, :] = p.astype(bf16)
            hm_ref[h] = top
            out = dot(e_ref[0, h], vg)
            inv = 1.0 / jnp.concatenate(sums, axis=0)
            here = iota((WIN, GRP * HD), 1) // HD == hh
            inv = jnp.broadcast_to(inv, (WIN, GRP * HD))
            if hh == 0:
                total, scale = out * inv, inv
            else:
                total = jnp.where(here, out * inv, total)
                scale = jnp.where(here, inv, scale)
        att_ref[:, pl.ds(off, GRP * HD)] = total.astype(bf16)
        linv_ref[:, pl.ds(off, GRP * HD)] = scale
        return carry

    lax.fori_loop(0, HEADS // GRP, group, 0)
    mid_ref[...] = xc_ref[...].astype(f32) + (dot(att_ref[...], wo_ref[...], NT) + bo_ref[...])
    for at, size in ROW_CHUNKS:
        centered, rstd = moments(mid_ref[at : at + size, :])
        n2_ref[at : at + size, :] = (centered * rstd * g2[...] + s2[...]).astype(bf16)


def gelu_both(hidden):
    z = jnp.abs(hidden) * (0.5**0.5)
    t = 1.0 / (1.0 + 0.3275911 * z)
    poly = 1.061405429
    for coefficient in (-1.453152027, 1.421413741, -0.284496736, 0.254829592):
        poly = poly * t + coefficient
    bell = jnp.exp2(hidden * hidden * (-0.5 * LOG2E))
    tail = 0.5 * poly * t * bell
    cdf = jnp.where(hidden >= 0.0, 1.0 - tail, tail)
    return hidden * cdf, cdf + hidden * bell * (1.0 / math.sqrt(2.0 * math.pi))


FC = 512


def feed_kernel(
    kr, kc, mid_ref, n2_ref, cot_ref, we_ref, be_ref, wr_ref, br_ref, g2,
    out_ref, mgrad_ref, dwe_ref, dwr_ref, dbe_ref, vec_ref,
    cc_scr, cT_scr, nT_scr, acc_scr, ng_scr,
):
    w = pl.program_id(0)

    @pl.when(w == 0)
    def _():
        dwe_ref[...] = jnp.zeros_like(dwe_ref)
        dwr_ref[...] = jnp.zeros_like(dwr_ref)
        dbe_ref[...] = jnp.zeros_like(dbe_ref)
        vec_ref[...] = jnp.zeros_like(vec_ref)

    canon = dot(picks_in(kr[0]), cot_ref[...])
    cc_scr[...] = canon.astype(bf16)
    cT_scr[...] = cc_scr[...].T
    nT_scr[...] = n2_ref[...].T

    def block(c, carry):
        off = pl.multiple_of(c * FC, FC)
        cols = pl.ds(off, FC)
        we = we_ref[:, cols]
        wr = wr_ref[:, cols]
        hidden = dot(n2_ref[...], we) + be_ref[:, cols]
        act, slope = gelu_both(hidden)
        act = act.astype(bf16)
        hg = (dot(cc_scr[...], wr) * slope).astype(bf16)
        feed = dot(act, wr, NT)
        back = dot(hg, we, NT)

        @pl.when(c == 0)
        def _():
            acc_scr[...] = feed
            ng_scr[...] = back

        @pl.when(c > 0)
        def _():
            acc_scr[...] += feed
            ng_scr[...] += back

        dwr_ref[:, cols] += dot(cT_scr[...], act)
        dwe_ref[:, cols] += dot(nT_scr[...], hg)
        dbe_ref[:, cols] += jnp.sum(hg.astype(f32), axis=0, keepdims=True)
        return carry

    lax.fori_loop(0, FF // FC, block, 0)
    for at, size in ROW_CHUNKS:
        rows = slice(at, at + size)
        mid = mid_ref[rows, :]
        cot = cc_scr[rows, :].astype(f32)
        acc_scr[rows, :] = mid + (acc_scr[rows, :] + br_ref[...])
        back = ng_scr[rows, :]
        centered, rstd = moments(mid)
        xhat = centered * rstd
        g = back * g2[...]
        mg = cot + rstd * (
            g - jnp.mean(g, axis=-1, keepdims=True) - xhat * jnp.mean(g * xhat, axis=-1, keepdims=True)
        )
        mgrad_ref[rows, :] = mg
        vec_ref[0:1, :] += jnp.sum(back * xhat, axis=0, keepdims=True)
        vec_ref[1:2, :] += jnp.sum(back, axis=0, keepdims=True)
        vec_ref[2:3, :] += jnp.sum(cot, axis=0, keepdims=True)
        vec_ref[3:4, :] += jnp.sum(mg.astype(bf16).astype(f32), axis=0, keepdims=True)
    out_ref[...] = dot(picks_out(kc[0]), acc_scr[...].astype(bf16)).astype(bf16)


def back_kernel(
    kc, xc_ref, nrm_ref, qkv_ref, e_ref, linv_ref, att_ref, mg_ref, w_ref, wo_ref, g1,
    out_ref, dw_ref, dwo_ref, db_ref, vec_ref, flat_ref,
    ag_scr, dop_scr, doT_scr, qT_scr, in_scr, x_scr, ds_scr, pg_scr, dvT_scr, dkT_scr, table_scr,
    seg_scr, wide_scr, grad_scr,
):
    w = pl.program_id(0)
    last = pl.num_programs(0) - 1

    @pl.when(w == 0)
    def _():
        dw_ref[...] = jnp.zeros_like(dw_ref)
        dwo_ref[...] = jnp.zeros_like(dwo_ref)
        db_ref[...] = jnp.zeros_like(db_ref)
        vec_ref[...] = jnp.zeros_like(vec_ref)
        table_scr[...] = jnp.zeros_like(table_scr)

    ag_scr[...] = mg_ref[...].astype(bf16)
    dwo_ref[...] += dot(ag_scr[...].T, att_ref[...])
    scaled = dot(ag_scr[...], wo_ref[...]).astype(bf16).astype(f32) * linv_ref[...]
    dop_scr[...] = scaled.astype(bf16)
    in_scr[...] = dop_scr[...].astype(f32) * att_ref[...].astype(f32)
    doT_scr[...] = dop_scr[...].T
    qT_scr[...] = qkv_ref[:, 0:D].T

    def group(g, carry):
        off = pl.multiple_of(g * (GRP * HD), GRP * HD)
        kg = qkv_ref[:, pl.ds(D + off, GRP * HD)]
        vg = qkv_ref[:, pl.ds(2 * D + off, GRP * HD)]
        dg = dop_scr[:, pl.ds(off, GRP * HD)]
        ig = in_scr[:, pl.ds(off, GRP * HD)]
        total = None
        for hh in range(GRP):
            h = g * GRP + hh
            lanes = head_lanes(hh)
            slot = x_scr.at[hh % 2]
            dslot = ds_scr.at[hh % 2]
            slot[...] = dot(dg * lanes, vg, NT)
            inner = jnp.sum(jnp.where(iota((WIN, GRP * HD), 1) // HD == hh, ig, 0.0), axis=1, keepdims=True)
            for at, size in ROW_CHUNKS:
                rows = slice(at, at + size)
                ds = (e_ref[0, h, rows, :].astype(f32) * (slot[rows, :] - inner[rows, :])).astype(bf16)
                dslot[rows, :] = ds
                table_scr[h, rows, :] += ds.astype(f32)
            hrow = pl.ds(pl.multiple_of(off + hh * HD, HD), HD)
            dvT_scr[hrow, :] = dot(doT_scr[hrow, :], e_ref[0, h]).astype(bf16)
            dkT_scr[hrow, :] = (dot(qT_scr[hrow, :], dslot[...]) * SCALE).astype(bf16)
            part = dot(dslot[...], kg * lanes)
            total = part if total is None else total + part
        pg_scr[:, pl.ds(off, GRP * HD)] = (total * SCALE).astype(bf16)
        return carry

    lax.fori_loop(0, HEADS // GRP, group, 0)
    pg_scr[:, D : 2 * D] = dkT_scr[...].T
    pg_scr[:, 2 * D :] = dvT_scr[...].T
    nT = nrm_ref[...].T
    for part in range(3):
        cols = slice(part * D, (part + 1) * D)
        dw_ref[:, cols] += dot(nT, pg_scr[:, cols])
        db_ref[:, cols] += jnp.sum(pg_scr[:, cols].astype(f32), axis=0, keepdims=True)
    grad_scr[...] = dot(pg_scr[...], w_ref[...], NT)
    for at, size in ROW_CHUNKS:
        rows = slice(at, at + size)
        back = grad_scr[rows, :]
        centered, rstd = moments(xc_ref[rows, :].astype(f32))
        xhat = centered * rstd
        g = back * g1[...]
        vec_ref[0:1, :] += jnp.sum(back * xhat, axis=0, keepdims=True)
        vec_ref[1:2, :] += jnp.sum(back, axis=0, keepdims=True)
        ag_scr[rows, :] = (
            mg_ref[rows, :]
            + rstd * (g - jnp.mean(g, axis=-1, keepdims=True) - xhat * jnp.mean(g * xhat, axis=-1, keepdims=True))
        ).astype(bf16)
    out_ref[...] = dot(picks_out(kc[0]), ag_scr[...]).astype(bf16)

    @pl.when(w == last)
    def _():
        spread = one_hot_flat()
        seg_scr[...] = jnp.zeros_like(seg_scr)
        flat_ref[...] = jnp.zeros_like(flat_ref)
        for wi in range(WW):
            total = None
            for hi in range(WH):
                at = (hi * WW + wi) * WT
                off = (WH - 1 - hi) * WW * WT
                seg_scr[:, 0:WIN] = table_scr[:, at : at + WT, :].reshape(HEADS * WT, WIN)
                moved = seg_scr[...]
                if off:
                    moved = pltpu.roll(moved, off, 1)
                total = moved if total is None else total + moved
            top = total.astype(bf16)
            low = (total - top.astype(f32)).astype(bf16)
            flat = dot(top, spread, NT) + dot(low, spread, NT)
            shift = (WW - 1 - wi) * WT
            flat_ref[...] += pltpu.roll(flat, shift, 1) if shift else flat


def whole(shape):
    return pl.BlockSpec(shape, lambda w: (0,) * len(shape))


def kept(shape):
    return pl.BlockSpec(shape, lambda w: (0,) * len(shape), pipeline_mode=pl.Buffered(1))


def per(shape):
    rest = (0,) * (len(shape) - 1)
    return pl.BlockSpec(shape, lambda w: (w,) + rest)


def shape_of(shape, dtype):
    return jax.ShapeDtypeStruct(shape, dtype)


PARAMS = pltpu.CompilerParams(dimension_semantics=("arbitrary",), vmem_limit_bytes=VMEM_LIMIT)


def run_attend(nw, kr, kc, rr, rc, x, w, wb, bias, wo, bo, g1, s1, g2, s2):
    rows = nw * WIN
    tok = per((WIN, D))
    return pl.pallas_call(
        attend_kernel,
        grid=(nw,),
        in_specs=[
            per((1, 1, WIN)), per((1, WIN, 1)), per((1, 1, WIN)), per((1, WIN, 1)), tok,
            kept((D, 3 * D)), kept((1, 3 * D)), kept((HEADS, WIN, WIN)), kept((D, D)),
            kept((1, D)), kept((1, D)), kept((1, D)), kept((1, D)), kept((1, D)),
        ],
        out_specs=[
            tok, tok, per((WIN, 3 * D)), per((1, HEADS, WIN, WIN)), tok, tok, tok, tok,
            whole((HEADS, 8, WIN)),
        ],
        out_shape=[
            shape_of((rows, D), bf16),
            shape_of((rows, D), bf16),
            shape_of((rows, 3 * D), bf16),
            shape_of((nw, HEADS, WIN, WIN), bf16),
            shape_of((rows, D), f32),
            shape_of((rows, D), bf16),
            shape_of((rows, D), f32),
            shape_of((rows, D), bf16),
            shape_of((HEADS, 8, WIN), f32),
        ],
        scratch_shapes=[pltpu.VMEM((2, WIN, WIN), f32), pltpu.VMEM((WIN, WIN), f32)],
        compiler_params=PARAMS,
        name="attend",
    )(kr, kc, rr, rc, x, w, wb, bias, wo, bo, g1, s1, g2, s2)


def run_feed(nw, kr, kc, mid, n2, cot, we, be, wr, br, g2):
    rows = nw * WIN
    tok = per((WIN, D))
    return pl.pallas_call(
        feed_kernel,
        grid=(nw,),
        in_specs=[
            per((1, 1, WIN)), per((1, WIN, 1)), tok, tok, tok,
            kept((D, FF)), kept((1, FF)), kept((D, FF)), kept((1, D)), kept((1, D)),
        ],
        out_specs=[tok, tok, whole((D, FF)), whole((D, FF)), whole((1, FF)), whole((8, D))],
        out_shape=[
            shape_of((rows, D), bf16),
            shape_of((rows, D), f32),
            shape_of((D, FF), f32),
            shape_of((D, FF), f32),
            shape_of((1, FF), f32),
            shape_of((8, D), f32),
        ],
        scratch_shapes=[
            pltpu.VMEM((WIN, D), bf16),
            pltpu.VMEM((D, WIN), bf16),
            pltpu.VMEM((D, WIN), bf16),
            pltpu.VMEM((WIN, D), f32),
            pltpu.VMEM((WIN, D), f32),
        ],
        compiler_params=PARAMS,
        name="feed",
    )(kr, kc, mid, n2, cot, we, be, wr, br, g2)


def run_back(nw, kc, xc, nrm, qkv, e, linv, att, mg, w, wo, g1):
    rows = nw * WIN
    tok = per((WIN, D))
    return pl.pallas_call(
        back_kernel,
        grid=(nw,),
        in_specs=[
            per((1, WIN, 1)), tok, tok, per((WIN, 3 * D)), per((1, HEADS, WIN, WIN)), tok, tok, tok,
            kept((D, 3 * D)), kept((D, D)), kept((1, D)),
        ],
        out_specs=[
            tok, whole((D, 3 * D)), whole((D, D)), whole((1, 3 * D)), whole((8, D)),
            whole((HEADS * WT, FLAT_PAD)),
        ],
        out_shape=[
            shape_of((rows, D), bf16),
            shape_of((D, 3 * D), f32),
            shape_of((D, D), f32),
            shape_of((1, 3 * D), f32),
            shape_of((8, D), f32),
            shape_of((HEADS * WT, FLAT_PAD), f32),
        ],
        scratch_shapes=[
            pltpu.VMEM((WIN, D), bf16),
            pltpu.VMEM((WIN, D), bf16),
            pltpu.VMEM((D, WIN), bf16),
            pltpu.VMEM((D, WIN), bf16),
            pltpu.VMEM((WIN, D), f32),
            pltpu.VMEM((2, WIN, WIN), f32),
            pltpu.VMEM((2, WIN, WIN), bf16),
            pltpu.VMEM((WIN, 3 * D), bf16),
            pltpu.VMEM((D, WIN), bf16),
            pltpu.VMEM((D, WIN), bf16),
            pltpu.VMEM((HEADS, WIN, WIN), f32),
            pltpu.VMEM((HEADS * WT, WIDE_PAD), f32),
            pltpu.VMEM((8, 128), f32),
            pltpu.VMEM((WIN, D), f32),
        ],
        compiler_params=PARAMS,
        name="attend_back",
    )(kc, xc, nrm, qkv, e, linv, att, mg, w, wo, g1)


BOTH = ("wide", "tensor")


def body(
    inputs, cotangent, window_order, region_ids, clip_threshold, norm1_gain, norm1_shift,
    qkv_weight, qv_bias, rel_table, out_weight, out_bias, norm2_gain, norm2_shift,
    expand_weight, expand_bias, reduce_weight, reduce_bias,
):
    parts = lax.axis_size("tensor")
    groups = lax.axis_size("wide")
    mine = lax.axis_index("tensor")
    own = HEADS // parts
    nw = inputs.shape[0] // WIN
    strip = D // groups

    order = lax.dynamic_slice_in_dim(window_order, mine * nw, nw, 0)
    place = order % SP * WT + order // SP
    regions = lax.dynamic_slice_in_dim(region_ids, mine * nw * WIN, nw * WIN, 0)
    regions = regions.reshape(nw, WIN).astype(f32)
    kr, kc = place[:, None, :], place[:, :, None]
    rr, rc = regions[:, None, :], regions[:, :, None]

    def row(v):
        return v.astype(f32)[None]

    qkv_strip = qkv_weight.reshape(strip, own, 3, HD).transpose(0, 2, 1, 3).reshape(strip, 3 * own * HD)
    shard = jnp.concatenate([qkv_strip, out_weight.T, expand_weight, reduce_weight.T], axis=1)
    full = lax.all_gather(shard, BOTH, axis=0)
    full = full.reshape(groups, parts, strip, shard.shape[1]).transpose(0, 2, 1, 3)
    full = full.reshape(D, parts, shard.shape[1])
    oc, fc = D // parts, FF // parts
    wqkv = full[:, :, : 3 * oc].reshape(D, parts, 3, oc).transpose(0, 2, 1, 3).reshape(D, 3 * D)
    wo = full[:, :, 3 * oc : 4 * oc].reshape(D, D)
    we = full[:, :, 4 * oc : 4 * oc + fc].reshape(D, FF)
    wr = full[:, :, 4 * oc + fc :].reshape(D, FF)
    small = jnp.concatenate([qv_bias.reshape(-1), expand_bias, rel_table.reshape(-1)])
    small = lax.all_gather(small, "tensor", axis=0)
    qv = small[:, : 2 * oc].reshape(parts, 2, oc).transpose(1, 0, 2).reshape(2, D).astype(f32)
    be = small[:, 2 * oc : 2 * oc + fc].reshape(1, FF).astype(f32)
    table = small[:, 2 * oc + fc :].reshape(HEADS, RT)
    wb = jnp.concatenate([qv[0:1], jnp.zeros((1, D), f32), qv[1:2]], axis=1)

    bias = table_bias(table)
    xc, nrm, qkv, e, linv, att, mid, n2, hm = run_attend(
        nw, kr, kc, rr, rc, inputs, wqkv, wb, bias, wo, row(out_bias),
        row(norm1_gain), row(norm1_shift), row(norm2_gain), row(norm2_shift),
    )
    layer_out, mg, dwe, dwr, dbe, vec2 = run_feed(
        nw, kr, kc, mid, n2, cotangent, we, be, wr, row(reduce_bias), row(norm2_gain)
    )
    input_grad, dw, dwo, db, vec1, flat = run_back(
        nw, kc, xc, nrm, qkv, e, linv, att, mg, wqkv, wo, row(norm1_gain)
    )

    grads = jnp.concatenate(
        [
            dw.reshape(D, 3, parts, oc).transpose(2, 0, 1, 3).reshape(parts, D, 3 * oc),
            dwo.reshape(D, parts, oc).transpose(1, 0, 2),
            dwe.reshape(D, parts, fc).transpose(1, 0, 2),
            dwr.reshape(D, parts, fc).transpose(1, 0, 2),
        ],
        axis=2,
    )
    grads = grads.reshape(parts, groups, strip, shard.shape[1]).transpose(1, 0, 2, 3)
    grads = grads.reshape(groups * parts * strip, shard.shape[1])
    mine_grad = lax.psum_scatter(grads, BOTH, scatter_dimension=0, tiled=True)
    qkv_out = (
        mine_grad[:, : 3 * oc].reshape(strip, 3, own, HD).transpose(0, 2, 1, 3).reshape(strip, 3 * oc)
    )
    out_out = mine_grad[:, 3 * oc : 4 * oc].T
    expand_out = mine_grad[:, 4 * oc : 4 * oc + fc]
    reduce_out = mine_grad[:, 4 * oc + fc :].T

    table_grad = table_back(flat)
    bias_grad = jnp.concatenate([db[:, :D], db[:, 2 * D :]], axis=0)
    sums = lax.psum((vec1[:2], vec2[:4], dbe, bias_grad, table_grad), BOTH)
    v1, v2, dbe_all, bias_all, table_all = sums
    peak = lax.pmax(jnp.max(hm, axis=(1, 2)) * SCALE, BOTH)
    start = mine * own
    peak_own = lax.dynamic_slice_in_dim(peak, start, own, 0)
    factor = jnp.sqrt(clip_threshold / jnp.maximum(peak_own, clip_threshold))
    column_factor = jnp.stack([factor, factor, jnp.ones_like(factor)], axis=1)
    clipped_qkv = (
        qkv_weight.astype(f32).reshape(strip, own, 3, HD) * column_factor[None, :, :, None]
    ).reshape(qkv_weight.shape)
    bias_scale = jnp.stack([jnp.repeat(factor, HD), jnp.ones((own * HD,), f32)], axis=0)
    clipped_bias = qv_bias.astype(f32) * bias_scale
    return (
        layer_out,
        input_grad,
        v1[0],
        v1[1],
        qkv_out,
        lax.dynamic_slice_in_dim(bias_all, start * HD, oc, 1),
        lax.dynamic_slice_in_dim(table_all, start, own, 0),
        out_out,
        v2[3],
        v2[0],
        v2[1],
        expand_out,
        lax.dynamic_slice_in_dim(dbe_all[0], mine * fc, fc, 0),
        reduce_out,
        v2[2],
        peak_own,
        clipped_qkv,
        clipped_bias,
    )


def solution(mesh):
    tokens = P(BOTH, None)
    in_specs = (
        tokens, tokens, P("wide", None), P("wide"), P(), P(), P(), P("wide", "tensor"),
        P(None, "tensor"), P("tensor", None), P("tensor", "wide"), P(), P(), P(),
        P("wide", "tensor"), P("tensor"), P("tensor", "wide"), P(),
    )
    out_specs = (
        tokens, tokens, P(), P(), P("wide", "tensor"), P(None, "tensor"), P("tensor", None),
        P("tensor", "wide"), P(), P(), P(), P("wide", "tensor"), P("tensor"),
        P("tensor", "wide"), P(), P("tensor"), P("wide", "tensor"), P(None, "tensor"),
    )
    return jax.shard_map(body, mesh=mesh, in_specs=in_specs, out_specs=out_specs, check_vma=False)
```

time: 2590 us -> 671 us (0.26)
  other arithmetic: 978 us -> 22.7 us
  local copies, waits for them, and re-layouts: 671 us -> 119 us
  matrix products: 312 us -> 0 us
  waiting for transfers between devices: 433 us -> 219 us
  Pallas kernels: 0 us -> 202 us
  blocking collectives: 167 us -> 79.6 us
    scatter-add x1 -> x0, other arithmetic: 819 us -> none  [body(): jax.ops.segment_sum(table_sum.reshape(heads, WIN * WIN).T, canon_index.re...]
    gather x12 -> x0, local copies, waits for them, and re-layouts: 528 us -> none  [the longest x2 334 us: body(): bias = jnp.take(table_use.astype(jnp.float32), canon_index, axis=1)]
    dot_general x68 -> x0, matrix products: 312 us -> none  [the longest x16 83.5 us: window_scores(): jnp.einsum('hqd,hkd->hqk', query_win, key_win, preferred_element_type=jnp...]
    pallas_call x0 -> x4, Pallas kernels: none -> 202 us  [the longest x1 75.6 us: run_back(): pl.pallas_call(back_kernel, grid=(nw,), in_specs=[per((1, WIN, 1)), tok,...]
    reduce_scatter x8 -> x1, waiting for transfers between devices: 331 us -> 161 us  [body(): mine_grad = lax.psum_scatter(grads, BOTH, scatter_dimension=0, tiled=True)]
    add x9 -> x2, other arithmetic: 92.8 us -> 5.45 us  [the longest x1 5.43 us: table_back(): total + jnp.pad(parts[:, :, :, tj], ((0, 0), (low, WT - 1 - low), (0, 0)))]
    all_gather x2 -> x0, blocking collectives: 84 us -> none  [the longest x1 43.9 us: body(): lax.all_gather(out_weight, 'wide', axis=1, tiled=True)]
    all_gather x6 -> x1, waiting for transfers between devices: 99.8 us -> 22.4 us  [body(): full = lax.all_gather(shard, BOTH, axis=0)]
  transfers between devices with their start and end apart: 15 -> 4, of which waited for: 12 -> 4; matrix products, arithmetic and copies ran while one was open for 21% -> 7% of each run, Pallas kernels for 0% -> 2%
where the time goes in v1:
time: 671 us; the launch traced here: 661 us
  waiting for transfers between devices  219 us (33%)
  Pallas kernels  202 us (30%)
  local copies, waits for them, and re-layouts  119 us (18%)
  blocking collectives  79.6 us (12%)
  other arithmetic  22.7 us (3%)
  between operations  18 us (3%)
    reduce_scatter x1, waiting for transfers between devices, body(): mine_grad = lax.psum_scatter(grads, BOTH, scatter_dimension=0, tiled=True)  161 us
    pallas_call x1, Pallas kernels, run_back(): pl.pallas_call(back_kernel, grid=(nw,), in_specs=[per((1, WIN, 1)), tok,...  75.6 us
    pallas_call x1, Pallas kernels, run_attend(): pl.pallas_call(attend_kernel, grid=(nw,), in_specs=[per((1, 1, WIN)), per...  62.6 us
    pallas_call x1, Pallas kernels, run_feed(): pl.pallas_call(feed_kernel, grid=(nw,), in_specs=[per((1, 1, WIN)), per((...  50.8 us
    psum x1, blocking collectives, body(): sums = lax.psum((vec1[:2], vec2[:4], dbe, bias_grad, table_grad), BOTH)  40.3 us
    pmax x1, blocking collectives, body(): peak = lax.pmax(jnp.max(hm, axis=(1, 2)) * SCALE, BOTH)  39.3 us
    psum x1, waiting for transfers between devices, body(): sums = lax.psum((vec1[:2], vec2[:4], dbe, bias_grad, table_grad), BOTH)  25.8 us
    all_gather x1, waiting for transfers between devices, body(): full = lax.all_gather(shard, BOTH, axis=0)  22.4 us
  transfers between devices with their start and end apart: 4, of which 4 were waited for; matrix products, arithmetic and copies ran while one was open for 7% of the time, Pallas kernels for 2%

profile of v1, /device:TPU:0, one launch (start us, length us, event | category | flops | bytes accessed | tf_op | source)
XLA Modules:
  0.0 660.6 jit_solution(1365129392235330072)
XLA Ops:
  8.8 0.9 reshape.168
  9.8 1.2 dynamic-slice.1
  13.7 1.0 reshape.161
  14.9 1.6 pad_maximum_fusion.1
  17.3 1.6 convert_element_type.93.rc
  23.0 1.2 copy.132.kc
  24.2 9.9 %all-reduce.17.cloned.1.call-done = bf16[43632]{0:T(1024)(128)(2,1)} async-done(((bf16[43632]{0:T(1024)(128)(2,1)}), bf16[43632]{0:T(1024)(128)(2,1)}) %all-reduce.17.cloned.1.call-update) | async-done | bytes 87280
  34.2 1.1 reshape.192
  38.8 5.9 copy.151
  44.7 8.3 %reshape.199 = f32[128,1352]{1,0:T(8,128)S(1)} reshape(f32[16,8,169,8]{3,2,1,0:T(8,128)} %copy.151) | data formatting | bytes 1384448 | tf_op jit(solution)/shard_map/reshape | solution.py:109
  53.0 0.9 pad.37.flat_ref
  53.9 12.7 %table_bias.1.bias_ref = f32[16,392,392]{2,1,0:T(8,128)} custom-call(f32[128,1408]{1,0:T(8,128)} %pad.37.flat_ref), custom_call_target="tpu_custom_call" | custom-call | tf_op jit(solution)/shard_map/table_bias/pallas_call | solution.py:111
  67.2 22.4 %all-gather.4.cloned.1.call-done = bf16[1024,3072]{1,0:T(8,128)(2,1)} async-done(((bf16[32,3072]{1,0:T(8,128)(2,1)}), bf16[1024,3072]{1,0:T(8,128)(2,1)}) %all-gather.4.cloned.1.call-update) | async-done | bytes 6291472 | tf_op jit(solution)/shard_map/all_gather | solution.py:525
  89.7 3.2 copy.121
  93.0 1.3 slice.200
  94.7 0.8 copy.160
  95.5 1.5 copy.162
  97.0 2.6 copy.122
  99.6 4.9 copy.123
  104.5 5.1 reshape.166.w_ref
  109.6 1.6 copy.161
  111.2 62.6 %attend.1 = (bf16[1568,512]{1,0:T(8,128)(2,1)}, bf16[1568,512]{1,0:T(8,128)(2,1)}, bf16[1568,1536]{1,0:T(8,128)(2,1)}, bf16[4,16,392,392]{3,2,1,0:T(8,128)(2,1)}...) custom-call(s32[4,1,392]{2,1,0:T(1,128)} %broadcast_in_dim.47.kr, ...), custom_call_target="tpu_custom_call" | custom-call | tf_op jit(solution)/shard_map/attend/pallas_call | solution.py:395
  173.8 50.8 %feed.1 = (bf16[1568,512]{1,0:T(8,128)(2,1)}, f32[1568,512]{1,0:T(8,128)}, f32[512,2048]{1,0:T(8,128)}, f32[512,2048]{1,0:T(8,128)}, f32[1,2048]{1,0:T(1,128)}, /*index=5*/f32[8,512]{1,0:T(8,128)}) custom-call(s32[4,1,392]{2,1,0:T(1,128)} %broadcast_in_dim.47.kr, s32[4,392,1]{2,1,0:T(8,128)} %copy.132.kc, f32[1568,512]{1,0:T(8,128)} %get-tuple-element.39.mid_ref, ...), custom_call_target="tpu_custom_call" | custom-call | tf_op jit(solution)/shard_map/feed/pallas_call | solution.py:427
  224.6 75.6 %attend_back.1 = (bf16[1568,512]{1,0:T(8,128)(2,1)}, f32[512,1536]{1,0:T(8,128)}, f32[512,512]{1,0:T(8,128)}, f32[1,1536]{1,0:T(1,128)}, f32[8,512]{1,0:T(8,128)}, /*index=5*/f32[128,1408]{1,0:T(8,128)}) custom-call(s32[4,392,1]{2,1,0:T(8,128)} %copy.132.kc, bf16[1568,512]{1,0:T(8,128)(2,1)} %get-tuple-element.42.xc_ref, ...), custom_call_target="tpu_custom_call" | custom-call | tf_op jit(solution)/shard_map/attend_back/pallas_call | solution.py:458
  300.2 2.3 copy.140
  303.1 1.1 copy.136
  304.3 3.8 reshape.173
  308.0 3.0 copy.171
  311.1 4.8 concatenate.27
  315.9 6.6 reshape.175
  322.5 5.4 copy.137
  327.9 6.7 %reshape.176 = f32[512,2,1024]{2,1,0:T(2,128)} reshape(f32[512,2048]{1,0:T(8,128)} %get-tuple-element.54) | data formatting | bytes 8388608 | tf_op jit(solution)/shard_map/reshape | solution.py:557
  334.6 5.4 copy.138
  340.0 8.8 %reshape.180 = f32[16,8,169,8]{1,0,3,2:T(8,128)} reshape(f32[128,1352]{0,1:T(8,128)} %copy.140) | data formatting | bytes 1384448 | tf_op jit(solution)/shard_map/reshape | solution.py:121
  348.8 6.8 %slice_bitcast_fusion.9 = (f32[16,8,169]{1,0,2:T(8,128)S(1)}, f32[16,8,169]{1,0,2:T(8,128)S(1)}, f32[16,8,169]{1,0,2:T(8,128)S(1)}, f32[16,8,169]{1,0,2:T(8,128)...) fusion(f32[16,8,169,8]{1,0,3,2:T(8,128)} %reshape.180), kind=kLoop, calls=%fused_computation.11 | loop fusion | bytes 1384448 | tf_op jit(solution)/shard_map/squeeze | solution.py:125
  355.6 5.4 pad_add_fusion
  361.0 2.5 rev.4
  363.5 2.0 copy.149
  365.5 0.8 reshape.181
  366.5 8.6 %pad_maximum_fusion = f32[2,16,32,3072]{3,2,0,1:T(8,128)} fusion(f32[2,16,32,1024]{3,2,0,1:T(8,128)} %copy.138, f32[2,16,32,1024]{3,2,0,1:T(8,128)} %copy.137, f32[2,16,32,256]{3,2,0,1:T(8,128)} %copy.136, f32[2,16,32,768]{3,2,1,0:T(8,128)S(1)} %concatenate.27), kind=kLoop, calls=%fused_computation | loop fusion | flops 9437184 | bytes 25165824 | tf_op jit(solution)/shard_map/concatenate | solution.py:552
  376.3 39.3 %pmax.7 = f32[16]{0:T(128)S(1)} all-reduce(f32[16]{0:T(128)S(1)} %broadcast_multiply_fusion), channel_id=1, replica_groups=mesh['wide'=16,'tensor'=2] {'wide','tensor'}, use_global_device_ids=true, to_apply=%region_7.8 | all-reduce | flops 16 | bytes 128 | tf_op jit(solution)/shard_map/pmax | solution.py:575
  416.6 0.7 slice.177
  417.4 40.3 %all-reduce.11 = (f32[2,512]{1,0:T(2,128)S(1)}, f32[2,512]{1,0:T(2,128)S(1)}, f32[4,512]{1,0:T(4,128)S(1)}, f32[1,2048]{1,0:T(1,128)S(1)}) all-reduce(f32[2,512]{1,0:T(2,128)S(1)} %slice.177, f32[2,512]{1,0:T(2,128)S(1)} %pad_maximum_fusion.3, f32[4,512]{1,0:T(4,128)S(1)} %slice.193, ...), channel_id=1, replica_groups=mesh['wide'=16,'tensor'=2] {'wide','tensor'}, use_global_device_ids=true, to_apply=%region_0.1 | all-reduce | flops 6144 | bytes 49152 | tf_op jit(solution)/shard_map/psum | solution.py:573
  460.7 25.8 %all-reduce.15.cloned.1.call-done = f32[16,2535]{1,0:T(8,128)} async-done(((f32[16,2535]{1,0:T(8,128)}), f32[16,2535]{1,0:T(8,128)}) %all-reduce.15.cloned.1.call-update) | async-done | bytes 162256 | tf_op jit(solution)/shard_map/psum | solution.py:573
  486.5 1.5 constant_dynamic-slice_fusion
  488.1 160.9 %reduce-scatter.2.cloned.1.call-done = f32[32,3072]{1,0:T(8,128)} async-done(((f32[1024,3072]{1,0:T(8,128)}), f32[32,3072]{1,0:T(8,128)}) %reduce-scatter.2.cloned.1.call-update) | async-done | bytes 393232 | tf_op jit(solution)/shard_map/reduce_scatter | solution.py:563
  649.0 1.0 slice.219
  650.2 1.0 reshape.179
  (113 shorter events, 19.2 us)
Async XLA Ops:
  8.0 8.5 %copy-start.7 = (s32[3136]{0:T(1024)S(1)}, s32[3136]{0:T(1024)}, u32[]{:S(2)}) copy-start(s32[3136]{0:T(1024)} %param.21) | copy-start | bytes 37636
  8.0 10.8 %copy-start.11 = (bf16[512]{0:T(512)(128)(2,1)S(1)}, bf16[512]{0:T(512)(128)(2,1)}, u32[]{:S(2)}) copy-start(bf16[512]{0:T(512)(128)(2,1)} %param.23) | copy-start | bytes 3076
  8.0 11.4 %copy-start.12 = (bf16[512]{0:T(512)(128)(2,1)S(1)}, bf16[512]{0:T(512)(128)(2,1)}, u32[]{:S(2)}) copy-start(bf16[512]{0:T(512)(128)(2,1)} %param.24) | copy-start | bytes 3076
  8.1 12.0 %copy-start.13 = (bf16[512]{0:T(512)(128)(2,1)S(1)}, bf16[512]{0:T(512)(128)(2,1)}, u32[]{:S(2)}) copy-start(bf16[512]{0:T(512)(128)(2,1)} %param.29) | copy-start | bytes 3076
  8.1 12.5 %copy-start.14 = (bf16[512]{0:T(512)(128)(2,1)S(1)}, bf16[512]{0:T(512)(128)(2,1)}, u32[]{:S(2)}) copy-start(bf16[512]{0:T(512)(128)(2,1)} %param.30) | copy-start | bytes 3076
  8.1 13.1 %copy-start.15 = (bf16[512]{0:T(512)(128)(2,1)S(1)}, bf16[512]{0:T(512)(128)(2,1)}, u32[]{:S(2)}) copy-start(bf16[512]{0:T(512)(128)(2,1)} %param.31) | copy-start | bytes 3076
  8.1 13.7 %copy-start.16 = (bf16[512]{0:T(512)(128)(2,1)S(1)}, bf16[512]{0:T(512)(128)(2,1)}, u32[]{:S(2)}) copy-start(bf16[512]{0:T(512)(128)(2,1)} %param.35) | copy-start | bytes 3076
  8.1 14.3 %copy-start.5 = (s32[8,392]{1,0:T(8,128)S(1)}, s32[8,392]{1,0:T(8,128)}, u32[]{:S(2)}) copy-start(s32[8,392]{1,0:T(8,128)} %param.20) | copy-start | bytes 37636
  8.1 26.1 %all-reduce.17.cloned.1.call-start = ((), (), s32[]{:S(2)}) async-start(), calls=%async_computation.4 | async-start | bytes 176128
  13.0 0.6 copy-start.2
  13.6 76.0 %all-gather.4.cloned.1.call-start = ((), (), s32[]{:S(2)}) async-start(), calls=%async_computation.3 | async-start | bytes 6488064 | tf_op jit(solution)/shard_map/all_gather | solution.py:525
  16.5 470.1 %all-reduce.15.cloned.1.call-start = ((), (), s32[]{:S(2)}) async-start(), calls=%async_computation.2 | async-start | bytes 327680 | tf_op jit(solution)/shard_map/psum | solution.py:573
  300.2 2.3 copy-start
  366.4 282.6 %reduce-scatter.2.cloned.1.call-start = ((), (), s32[]{:S(2)}) async-start(), calls=%async_computation.1 | async-start | bytes 12976128 | tf_op jit(solution)/shard_map/reduce_scatter | solution.py:563
  375.1 1.0 copy-start.3
  375.1 42.2 %copy-start.8 = (f32[8,512]{1,0:T(8,128)S(1)}, f32[8,512]{1,0:T(8,128)}, u32[]{:S(2)}) copy-start(f32[8,512]{1,0:T(8,128)} %get-tuple-element.57) | copy-start | bytes 49156
  375.1 42.2 %copy-start.10 = (f32[1,1536]{1,0:T(1,128)S(1)}, f32[1,1536]{1,0:T(1,128)}, u32[]{:S(2)}) copy-start(f32[1,1536]{1,0:T(1,128)} %get-tuple-element.55) | copy-start | bytes 18436
  375.1 42.3 %copy-start.6 = (f32[1,2048]{1,0:T(1,128)S(1)}, f32[1,2048]{1,0:T(1,128)}, u32[]{:S(2)}) copy-start(f32[1,2048]{1,0:T(1,128)} %get-tuple-element.58) | copy-start | bytes 24580
  375.1 83.8 %copy-start.9 = (bf16[2,256]{1,0:T(2,128)(2,1)S(1)}, bf16[2,256]{1,0:T(2,128)(2,1)}, u32[]{:S(2)}) copy-start(bf16[2,256]{1,0:T(2,128)(2,1)} %param.26) | copy-start | bytes 3076
  375.1 85.0 %copy-start.4 = (bf16[32,768]{1,0:T(8,128)(2,1)S(1)}, bf16[32,768]{1,0:T(8,128)(2,1)}, u32[]{:S(2)}) copy-start(bf16[32,768]{1,0:T(8,128)(2,1)} %param.25) | copy-start | bytes 147460
  649.0 2.3 copy-start.1
Sparse Core Ops, SparseCore 0:
  13.8 20.3 all-reduce.16
Sparse Core Ops, SparseCore 1:
  17.6 72.0 all-gather.3
  366.5 120.0 all-reduce.14
  492.4 156.5 reduce-scatter.1

commit v2 on v1

v2 whole, which is shorter than its diff:
```python
import functools
import math

import jax
import jax.numpy as jnp
from jax import lax
from jax.experimental import pallas as pl
from jax.experimental.pallas import tpu as pltpu
from jax.sharding import PartitionSpec as P

D = 512
HEADS = 16
HD = 32
FF = 2048
WT = 8
WH = 7
WW = 7
SP = WH * WW
WIN = 392
RT = 2535
ROWS = 13 * 13
GRP = 4

epsilon = 1e-05
masked = -100.0
lowest = -1e30
LOG2E = 1.4426950408889634
SCALE = HD ** (-0.5)
WIDE_SEG = 13 * WW * WT
WIDE_PAD = 768
PITCH = 176
FLAT_PAD = 1408
UP = 256
HALF = D // 2
QW = 3 * HALF
VW = QW + FF // 2

f32 = jnp.float32
bf16 = jnp.bfloat16
NN = (((1,), (0,)), ((), ()))
NT = (((1,), (1,)), ((), ()))
TN = (((0,), (0,)), ((), ()))

VMEM_LIMIT = 60 * 2**20


def dot(a, b, dims=NN):
    return lax.dot_general(a, b, dims, preferred_element_type=f32)


def chunks(total, size):
    starts = list(range(0, total - size + 1, size))
    sizes = [size] * len(starts)
    rest = total - size * len(starts)
    if rest:
        if rest < size // 2:
            sizes[-1] += rest
        else:
            starts.append(size * len(starts))
            sizes.append(rest)
    return list(zip(starts, sizes))


ROW_CHUNKS = chunks(WIN, 64)


def iota(shape, axis):
    return lax.broadcasted_iota(jnp.int32, shape, axis)


def group_at(g):
    return pl.multiple_of(g // 2 * QW + g % 2 * (GRP * HD), GRP * HD)


def head_lanes(hh):
    return (iota((1, GRP * HD), 1) // HD == hh).astype(f32).astype(bf16)


def picks_of(order_ref, w):
    order = order_ref[pl.ds(w, 1), :]
    return iota((WIN, WIN), 0) == order % SP * WT + order // SP


def one_hot(hit):
    return hit.astype(f32).astype(bf16)


def column_moves():
    new = iota((1, QW), 1)
    old = new % HALF // HD * (3 * HD) + new // HALF * HD + new % HD
    return one_hot(iota((QW, QW), 0) == old)


def moments(rows):
    mean = jnp.mean(rows, axis=-1, keepdims=True)
    centered = rows - mean
    spread = jnp.mean(centered * centered, axis=-1, keepdims=True)
    return centered, lax.rsqrt(spread + epsilon)


def one_hot_spread():
    column = iota((1, WIDE_PAD), 1)
    dh, rest = column // (WW * WT), column % (WW * WT)
    target = rest % WT * PITCH + (12 - dh) * 13 + 6 - rest // WT
    target = jnp.where(column < WIDE_SEG, target, -1)
    return (iota((FLAT_PAD, WIDE_PAD), 0) == target).astype(f32).astype(bf16)


def flatten_table(table_ref, flat_ref):
    total = None
    rest = jnp.zeros((HEADS * WT, FLAT_PAD - UP), f32)
    for tj in range(WT):
        rows = table_ref[:, WT - 1 - tj : 2 * WT - 1 - tj, :].reshape(HEADS * WT, UP)
        part = jnp.concatenate([rows, rest], axis=1)
        if tj:
            part = pltpu.roll(part, tj * PITCH, 1)
        total = part if total is None else total + part
    flat_ref[...] = total


def turn_table(flat_ref, wide_ref, out_ref):
    flat = flat_ref[...]
    for wi in range(WW):
        wide_ref[wi] = (pltpu.roll(flat, FLAT_PAD - wi, 1) if wi else flat).astype(bf16)
    out_ref[...] = dot(wide_ref[...].reshape(WW * HEADS * WT, FLAT_PAD), one_hot_spread()) * LOG2E


def spread_table(turned_ref, bias_ref):
    for wi in range(WW):
        for hi in range(WH):
            at = (hi * WW + wi) * WT
            off = (WH - 1 - hi) * WW * WT
            rows = turned_ref[wi * HEADS * WT : (wi + 1) * HEADS * WT, off : off + WIN]
            bias_ref[:, at : at + WT, :] = rows.reshape(HEADS, WT, WIN)


def table_kernel(table_ref, bias_ref, flat_ref, wide_ref, turned_ref):
    flatten_table(table_ref, flat_ref)
    turn_table(flat_ref, wide_ref, turned_ref)
    spread_table(turned_ref, bias_ref)


TABLE_SCRATCH = [
    pltpu.VMEM((HEADS * WT, FLAT_PAD), f32),
    pltpu.VMEM((WW, HEADS * WT, FLAT_PAD), bf16),
    pltpu.VMEM((WW * HEADS * WT, WIDE_PAD), f32),
]


def padded_table(table):
    parts = table.astype(f32).reshape(-1, 2 * WT - 1, ROWS)
    return jnp.pad(parts, ((0, 0), (0, 1), (0, UP - ROWS)))


def table_bias(table):
    return pl.pallas_call(
        table_kernel,
        out_shape=jax.ShapeDtypeStruct((HEADS, WIN, WIN), f32),
        scratch_shapes=TABLE_SCRATCH,
        compiler_params=pltpu.CompilerParams(vmem_limit_bytes=VMEM_LIMIT),
        name="table_bias",
    )(padded_table(table))


def fold_table(table_scr, seg_scr, wide_scr, out_ref):
    seg_scr[...] = jnp.zeros_like(seg_scr)
    for wi in range(WW):
        total = None
        for hi in range(WH):
            at = (hi * WW + wi) * WT
            off = (WH - 1 - hi) * WW * WT
            seg_scr[:, 0:WIN] = table_scr[:, at : at + WT, :].reshape(HEADS * WT, WIN)
            moved = seg_scr[...]
            if off:
                moved = pltpu.roll(moved, off, 1)
            total = moved if total is None else total + moved
        wide_scr[wi] = total.astype(bf16)
    flat = dot(wide_scr[...].reshape(WW * HEADS * WT, WIDE_PAD), one_hot_spread(), NT)
    total = None
    for wi in range(WW):
        part = flat[wi * HEADS * WT : (wi + 1) * HEADS * WT, :]
        part = pltpu.roll(part, wi, 1) if wi else part
        total = part if total is None else total + part
    out_ref[...] = jnp.zeros_like(out_ref)
    for tj in range(WT):
        rows = pltpu.roll(total, FLAT_PAD - tj * PITCH, 1) if tj else total
        out_ref[:, WT - 1 - tj : 2 * WT - 1 - tj, :] += rows[:, :UP].reshape(HEADS, WT, UP)


def attend_kernel(nb, order_ref, region_ref, x_ref, *rest):
    if nb:
        (params_ref, table_ref, own_ref), shards, rest = rest[:3], rest[3:6], rest[6:]
    else:
        (vecs_ref, w_ref, bias_ref), rest = rest[:3], rest[3:]
    (xc_ref, nrm_ref, qkv_ref, e_ref, linv_ref, att_ref, peak_ref), rest = rest[:7], rest[7:]
    if nb:
        (vecs_out, w_out), bufs, rest = rest[:2], rest[2:5], rest[5:]
    (x_scr, mask_scr, hm_ref), rest = rest[:3], rest[3:]
    w, g = pl.program_id(0), pl.program_id(1)
    at_step = w * (HEADS // GRP) + g
    opening = (w == 0) & (g == 0)
    if nb:
        (vecs_ref, w_scr, bias_ref, own_scr, tables, flat_ref, wide_ref, turned_ref), sems = rest[:8], rest[8:]
        place = Place(nb)
        first = Gather(place, [own_scr], [w_scr], *sems[:3])
        second = Gather(place, shards, bufs, *sems[3:])
        base = Gather.copies(nb, 1)
        mine = pl.ds(pl.multiple_of(place.t * (HEADS // 2), HEADS // 2), HEADS // 2)
        near = [
            remote(part, part, sems[0].at[base + i], sems[1].at[base + i], place.sibling())
            for i, part in enumerate((tables.at[mine], vecs_ref.at[place.t]))
        ]

    def prepare():
        pick = picks_of(order_ref, w)
        region = region_ref[pl.ds(w, 1), :]
        row_at = jnp.sum(jnp.where(pick, region, 0.0), axis=1, keepdims=True)
        pick = one_hot(pick)
        column_at = dot(jnp.broadcast_to(region, (8, WIN)).astype(bf16), pick, NT)[0:1, :]
        mask_scr[...] = jnp.where(row_at == column_at, 0.0, masked * LOG2E)
        xc_ref[...] = dot(pick, x_ref[...]).astype(bf16)
        for at, size in ROW_CHUNKS:
            centered, rstd = moments(xc_ref[at : at + size, :].astype(f32))
            nrm_ref[at : at + size, :] = (centered * rstd * vecs_ref[0, 1:2, 0:D] + vecs_ref[0, 2:3, 0:D]).astype(bf16)

    def project():
        weight = w_scr[...].reshape(D, 3 * D) if nb else w_ref
        for v in range(2):
            cols = slice(v * QW, (v + 1) * QW)
            qkv_ref[:, cols] = (dot(nrm_ref[...], weight[:, cols]) + vecs_ref[v, 0:1, 0:QW]).astype(bf16)

    def group():
        off = pl.multiple_of(g * (GRP * HD), GRP * HD)
        qoff = group_at(g)
        qg = qkv_ref[:, pl.ds(qoff, GRP * HD)]
        kg = qkv_ref[:, pl.ds(qoff + HALF, GRP * HD)]
        vg = qkv_ref[:, pl.ds(qoff + 2 * HALF, GRP * HD)]
        vx = jnp.concatenate([vg, jnp.ones((WIN, GRP * HD), bf16)], axis=1)

        def score(hh):
            x_scr[hh % 2] = dot(qg * head_lanes(hh), kg, NT)

        def soften(hh):
            h = g * GRP + hh
            top = hm_ref[h]
            for at, size in ROW_CHUNKS:
                xx = x_scr[hh % 2, at : at + size, :]
                top = jnp.maximum(top, jnp.max(xx.reshape(size // 8, 8, WIN), axis=0))
                s = xx * (SCALE * LOG2E) + bias_ref[h, at : at + size, :] + mask_scr[at : at + size, :]
                e_ref[0, hh, at : at + size, :] = jnp.exp2(s - jnp.max(s, axis=1, keepdims=True)).astype(bf16)
            hm_ref[h] = top

        def weigh(hh, total, scale):
            out = dot(e_ref[0, hh], vx)
            inv = 1.0 / out[:, GRP * HD :]
            out = out[:, : GRP * HD] * inv
            if hh == 0:
                return out, inv
            here = iota((WIN, GRP * HD), 1) // HD == hh
            return jnp.where(here, out, total), jnp.where(here, inv, scale)

        total = scale = None
        score(0)
        for hh in range(GRP):
            if hh + 1 < GRP:
                score(hh + 1)
            soften(hh)
            if hh:
                total, scale = weigh(hh - 1, total, scale)
        total, scale = weigh(GRP - 1, total, scale)
        att_ref[:, pl.ds(off, GRP * HD)] = total.astype(bf16)
        linv_ref[:, pl.ds(off, GRP * HD)] = scale

    @pl.when(opening)
    def _():
        hm_ref[...] = jnp.full(hm_ref.shape, lowest, f32)
        if nb:
            place.greet()
            own_scr[...] = dot(own_ref[...], column_moves()).astype(bf16)
            first.step(0)
            tables[mine] = table_ref[...]
            vecs_ref[place.t] = params_ref[...]
            for copy in near:
                copy.start()
            for copy in near:
                copy.wait()
            flatten_table(tables, flat_ref)
            first.step(1)

    @pl.when(g == 0)
    def _():
        prepare()

    if nb:

        @pl.when(opening)
        def _():
            first.step(2)
            turn_table(flat_ref, wide_ref, turned_ref)
            first.step(3)
            second.step(0)
            spread_table(turned_ref, bias_ref)
            for p in range(4, first.steps()):
                first.step(p)
            w_out[...] = w_scr[...].reshape(D, 3 * D)
            vecs_out[...] = vecs_ref[...]

        run_beside(second, at_step, GATHER_TIMES)

    @pl.when(g == 0)
    def _():
        project()

    group()

    @pl.when(at_step == pl.num_programs(0) * pl.num_programs(1) - 1)
    def _():
        lane = iota((1, D), 1)
        peaks = jnp.full((1, D), lowest, f32)
        for h in range(HEADS):
            top = jnp.max(jnp.max(hm_ref[h], axis=0, keepdims=True), axis=1, keepdims=True)
            peaks = jnp.where(lane == h, top * SCALE, peaks)
        peak_ref[...] = jnp.broadcast_to(peaks, peak_ref.shape)


def gelu_both(hidden):
    z = jnp.abs(hidden) * (0.5**0.5)
    base = 1.0 + 0.3275911 * z
    t = pl.reciprocal(base, approx=True)
    t = t * (2.0 - base * t)
    poly = 1.061405429
    for coefficient in (-1.453152027, 1.421413741, -0.284496736, 0.254829592):
        poly = poly * t + coefficient
    bell = jnp.exp2(hidden * hidden * (-0.5 * LOG2E))
    tail = 0.5 * poly * t * bell
    cdf = jnp.where(hidden >= 0.0, 1.0 - tail, tail)
    return hidden * cdf, cdf + hidden * bell * (1.0 / math.sqrt(2.0 * math.pi))


FC = 256
FEED_CHUNKS = chunks(WIN, 32)


def feed_kernel(
    order_ref, vecs_ref, xc_ref, att_ref, cot_ref, wo_ref, we_ref, wr_ref,
    out_ref, mgrad_ref, gwe_ref, gwr_ref, gwo_ref, vec_ref,
    mid_ref, n2_ref, cc_scr, cT_scr, nT_scr, acc_scr, ng_scr, dwe_ref, dwr_ref, dwo_ref,
    hid_scr, ag_scr, act_scr, hg_scr,
):
    w = pl.program_id(0)

    @pl.when(w == 0)
    def _():
        dwe_ref[...] = jnp.zeros_like(dwe_ref)
        dwr_ref[...] = jnp.zeros_like(dwr_ref)
        dwo_ref[...] = jnp.zeros_like(dwo_ref)
        vec_ref[...] = jnp.zeros_like(vec_ref)

    g2, s2, bo, br = (vecs_ref[0, i : i + 1, 0:D] for i in (3, 4, 5, 6))
    pick = one_hot(picks_of(order_ref, w))
    mid_ref[...] = xc_ref[...].astype(f32) + (dot(att_ref[...], wo_ref[...], NT) + bo)
    for at, size in ROW_CHUNKS:
        centered, rstd = moments(mid_ref[at : at + size, :])
        n2_ref[at : at + size, :] = (centered * rstd * g2 + s2).astype(bf16)
    canon = dot(pick, cot_ref[...])
    cc_scr[...] = canon.astype(bf16)
    cT_scr[...] = cc_scr[...].T
    nT_scr[...] = n2_ref[...].T

    blocks = [slice(c * FC, (c + 1) * FC) for c in range(FF // FC)]

    def widen(c):
        hid_scr[c % 2] = dot(n2_ref[...], we_ref[:, blocks[c]])
        ag_scr[c % 2] = dot(cc_scr[...], wr_ref[:, blocks[c]])

    def bend(c):
        half, off = divmod(c * FC, FF // 2)
        shift = vecs_ref[half, 0:1, QW + off : QW + off + FC]
        total = jnp.zeros((8, FC), f32)
        for at, size in FEED_CHUNKS:
            rows = slice(at, at + size)
            act, slope = gelu_both(hid_scr[c % 2, rows, :] + shift)
            act_scr[rows, blocks[c]] = act.astype(bf16)
            hg = (ag_scr[c % 2, rows, :] * slope).astype(bf16)
            hg_scr[rows, blocks[c]] = hg
            total += jnp.sum(hg.astype(f32).reshape(size // 8, 8, FC), axis=0)
        line, off = divmod(c * FC, D)
        vec_ref[4 + line : 5 + line, off : off + FC] += jnp.sum(total, axis=0, keepdims=True)

    def gather_up(c):
        dwr_ref[:, blocks[c]] += dot(cT_scr[...], act_scr[:, blocks[c]])
        dwe_ref[:, blocks[c]] += dot(nT_scr[...], hg_scr[:, blocks[c]])

    widen(0)
    for c in range(FF // FC):
        if c + 1 < FF // FC:
            widen(c + 1)
        bend(c)
        if c:
            gather_up(c - 1)
    gather_up(FF // FC - 1)
    acc_scr[...] = dot(act_scr[...], wr_ref[...], NT)
    ng_scr[...] = dot(hg_scr[...], we_ref[...], NT)
    for at, size in ROW_CHUNKS:
        rows = slice(at, at + size)
        mid = mid_ref[rows, :]
        cot = cc_scr[rows, :].astype(f32)
        acc_scr[rows, :] = mid + (acc_scr[rows, :] + br)
        back = ng_scr[rows, :]
        centered, rstd = moments(mid)
        xhat = centered * rstd
        g = back * g2
        mg = cot + rstd * (
            g - jnp.mean(g, axis=-1, keepdims=True) - xhat * jnp.mean(g * xhat, axis=-1, keepdims=True)
        )
        mgrad_ref[rows, :] = mg
        vec_ref[0:1, :] += jnp.sum(back * xhat, axis=0, keepdims=True)
        vec_ref[1:2, :] += jnp.sum(back, axis=0, keepdims=True)
        vec_ref[2:3, :] += jnp.sum(cot, axis=0, keepdims=True)
        vec_ref[3:4, :] += jnp.sum(mg.astype(bf16).astype(f32), axis=0, keepdims=True)
    out_ref[...] = dot(pick, acc_scr[...].astype(bf16), TN).astype(bf16)
    cT_scr[...] = mgrad_ref[...].astype(bf16).T
    dwo_ref[...] += dot(cT_scr[...], att_ref[...])

    @pl.when(w == pl.num_programs(0) - 1)
    def _():
        for grad, acc, width in ((gwe_ref, dwe_ref, FF // 2), (gwr_ref, dwr_ref, FF // 2), (gwo_ref, dwo_ref, HALF)):
            for v in range(2):
                for at in range(0, D, 64):
                    grad[v, at : at + 64, :] = acc[at : at + 64, v * width : (v + 1) * width].astype(bf16)


def back_kernel(
    nb, plans, order_ref, vecs_ref, xc_ref, nrm_ref, qkv_ref, e_ref, linv_ref, att_ref, mg_ref, w_ref, wo_ref,
    feed_ref, peak_ref, *rest
):
    if nb:
        matrices, rest = rest[:3], rest[3:]
        (out_ref, sums_out, table_out, qkv_out), outs, rest = rest[:4], rest[4:7], rest[7:]
    else:
        (out_ref, acc, table_out, gw_ref), rest = rest[:4], rest[4:]
    (
        dw_ref, wide_scr, ag_scr, dop_scr, doT_scr, qT_scr, in_scr, x_scr, ds_scr, pg_scr, dvT_scr, dkT_scr,
        table_scr, seg_scr, grad_scr,
    ), rest = rest[:15], rest[15:]
    w, g = pl.program_id(0), pl.program_id(1)
    end = HEADS // GRP - 1
    at_step = w * (HEADS // GRP) + g
    closing = at_step == pl.num_programs(0) * pl.num_programs(1) - 1
    if nb:
        (gw_ref, fold_scr, own_out, vec, vec_in, table, table_in), rest = rest[:7], rest[7:]
        acc = vec.at[0]
        place = Place(nb)
        count = [len(plan) * (nb + 2) for plan in plans]
        early, rest = rest[: count[0]], rest[count[0] :]
        late, sems = rest[: count[1]], rest[count[1] :]
        first = Scatter(place, build_streams(plans[0], matrices, early, outs, nb), *sems[:3])
        second = Scatter(place, build_streams(plans[1], [gw_ref], late, [own_out], nb), *sems[3:])
        sums = Sums(place, vec, vec_in, table, table_in, sems[3], sems[4], len(plans[1]) * (nb + 1))

    def prepare():
        ag_scr[...] = mg_ref[...].astype(bf16)
        scaled = dot(ag_scr[...], wo_ref[...]).astype(bf16).astype(f32) * linv_ref[...]
        dop_scr[...] = scaled.astype(bf16)
        in_scr[...] = (dop_scr[...].astype(f32) * -att_ref[...].astype(f32)).astype(bf16)
        doT_scr[...] = dop_scr[...].T
        for v in range(2):
            qT_scr[v * HALF : (v + 1) * HALF, :] = qkv_ref[:, v * QW : v * QW + HALF].T

    def group():
        off = pl.multiple_of(g * (GRP * HD), GRP * HD)
        qoff = group_at(g)
        kg = qkv_ref[:, pl.ds(qoff + HALF, GRP * HD)]
        vg = qkv_ref[:, pl.ds(qoff + 2 * HALF, GRP * HD)]
        vx = jnp.concatenate([vg, jnp.ones((WIN, GRP * HD), bf16)], axis=1)
        dx = jnp.concatenate([dop_scr[:, pl.ds(off, GRP * HD)], in_scr[:, pl.ds(off, GRP * HD)]], axis=1)

        def score(hh):
            lanes = head_lanes(hh)
            x_scr[hh % 2] = dot(dx * jnp.concatenate([lanes, lanes], axis=1), vx, NT)

        def differ(hh):
            h = g * GRP + hh
            for at, size in ROW_CHUNKS:
                rows = slice(at, at + size)
                ds = (e_ref[0, hh, rows, :].astype(f32) * x_scr[hh % 2, rows, :]).astype(bf16)
                ds_scr[hh % 2, rows, :] = ds
                table_scr[h, rows, :] += ds.astype(f32)

        def spread(hh, total):
            hrow = pl.ds(pl.multiple_of(off + hh * HD, HD), HD)
            ds = ds_scr[hh % 2]
            dvT_scr[hrow, :] = dot(doT_scr[hrow, :], e_ref[0, hh]).astype(bf16)
            dkT_scr[hrow, :] = (dot(qT_scr[hrow, :], ds) * SCALE).astype(bf16)
            part = dot(ds, kg * head_lanes(hh))
            return part if total is None else total + part

        total = None
        score(0)
        for hh in range(GRP):
            if hh + 1 < GRP:
                score(hh + 1)
            differ(hh)
            if hh:
                total = spread(hh - 1, total)
        total = spread(GRP - 1, total)
        pg_scr[:, pl.ds(qoff, GRP * HD)] = (total * SCALE).astype(bf16)

    def collect():
        for v in range(2):
            heads = slice(v * HALF, (v + 1) * HALF)
            pg_scr[:, v * QW + HALF : v * QW + 2 * HALF] = dkT_scr[heads, :].T
            pg_scr[:, v * QW + 2 * HALF : (v + 1) * QW] = dvT_scr[heads, :].T
        nT = nrm_ref[...].T
        for part in range(3):
            cols = slice(part * D, (part + 1) * D)
            dw_ref[:, cols] += dot(nT, pg_scr[:, cols])
            acc[10 + part : 11 + part, :] += jnp.sum(pg_scr[:, cols].astype(f32), axis=0, keepdims=True)

    def finish():
        grad_scr[...] = dot(pg_scr[...], w_ref[...], NT)
        for at, size in ROW_CHUNKS:
            rows = slice(at, at + size)
            back = grad_scr[rows, :]
            centered, rstd = moments(xc_ref[rows, :].astype(f32))
            xhat = centered * rstd
            g = back * vecs_ref[0, 1:2, 0:D]
            acc[0:1, :] += jnp.sum(back * xhat, axis=0, keepdims=True)
            acc[1:2, :] += jnp.sum(back, axis=0, keepdims=True)
            ag_scr[rows, :] = (
                mg_ref[rows, :]
                + rstd * (g - jnp.mean(g, axis=-1, keepdims=True) - xhat * jnp.mean(g * xhat, axis=-1, keepdims=True))
            ).astype(bf16)
        out_ref[...] = dot(one_hot(picks_of(order_ref, w)), ag_scr[...], TN).astype(bf16)

    @pl.when(at_step == 0)
    def _():
        dw_ref[...] = jnp.zeros_like(dw_ref)
        acc[...] = jnp.zeros((VEC_ROWS, D), f32)
        table_scr[...] = jnp.zeros_like(table_scr)
        if nb:
            place.greet()
            first.step(0)

    if nb:
        run_beside(first, at_step, SCATTER_TIMES)

    @pl.when(g == 0)
    def _():
        prepare()

    group()

    @pl.when(g == end)
    def _():
        collect()

    @pl.when(closing)
    def _():
        strip = D >> nb if nb else D
        for v in range(2):
            for at in range(0, D, 64):
                part = dw_ref[at : at + 64, v * QW : (v + 1) * QW].astype(bf16)
                if nb:
                    for i in range(64 // strip):
                        bits = tuple((at // strip + i) // (1 << k) % 2 for k in reversed(range(nb)))
                        gw_ref[(v, *bits)] = part[i * strip : (i + 1) * strip, :]
                else:
                    gw_ref[v, at : at + 64, :] = part
        if nb:
            second.step(0)

    @pl.when(g == end)
    def _():
        finish()

    @pl.when(closing)
    def _():
        acc[2:10, :] = feed_ref[...]
        acc[SUM_ROWS:VEC_ROWS, :] = peak_ref[...]
        if not nb:
            fold_table(table_scr, seg_scr, wide_scr, table_out)
            return
        second.step(1)
        for p in range(1, first.steps()):
            if SCATTER_TIMES[min(p, len(SCATTER_TIMES) - 1)] >= 1.0:
                first.step(p)
        fold_table(table_scr, seg_scr, wide_scr, fold_scr)
        half = HEADS // 2
        for v in range(2):
            table[v] = fold_scr[v * half : (v + 1) * half].astype(bf16)
        for p in range(second.steps()):
            sums.step(p, sums_out, table_out)
            if p + 2 < second.steps():
                second.step(p + 2)
        top = own_out[...].astype(bf16)
        low = (own_out[...] - top.astype(f32)).astype(bf16)
        moves = column_moves()
        qkv_out[...] = dot(top, moves, NT) + dot(low, moves, NT)


def whole(shape):
    return pl.BlockSpec(shape, lambda *at: (0,) * len(shape))


def kept(shape):
    return pl.BlockSpec(shape, lambda *at: (0,) * len(shape), pipeline_mode=pl.Buffered(1))


def per(shape):
    rest = (0,) * (len(shape) - 1)
    return pl.BlockSpec(shape, lambda w, *at: (w,) + rest)


EXPS = pl.BlockSpec((1, GRP, WIN, WIN), lambda w, g: (w, g, 0, 0))


def shape_of(shape, dtype):
    return jax.ShapeDtypeStruct(shape, dtype)


PARAMS = pltpu.CompilerParams(vmem_limit_bytes=VMEM_LIMIT)
ANY = pl.BlockSpec(memory_space=pl.ANY)
SUM_ROWS = 16
VEC_ROWS = 24


def dma(*counts):
    return [pltpu.SemaphoreType.DMA((n,)) for n in counts]


def run_attend(nw, nb, order, region, x, weights, shards):
    rows = nw * WIN
    tok = per((WIN, D))
    out_specs = [tok, tok, per((WIN, 3 * D)), EXPS, tok, tok, whole((8, D))]
    out_shape = [
        shape_of((rows, D), bf16),
        shape_of((rows, D), bf16),
        shape_of((rows, 3 * D), bf16),
        shape_of((nw, HEADS, WIN, WIN), bf16),
        shape_of((rows, D), f32),
        shape_of((rows, D), bf16),
        shape_of((8, D), f32),
    ]
    scratch = [pltpu.VMEM((2, WIN, WIN), f32), pltpu.VMEM((WIN, WIN), f32), pltpu.VMEM((HEADS, 8, WIN), f32)]
    if nb:
        strip = D >> nb
        copies, more = Gather.copies(nb, 1) + 2, Gather.copies(nb, len(shards))
        out_specs += [whole((2, 8, VW)), whole((D, 3 * D)), *[ANY] * len(shards)]
        out_shape += [shape_of((2, 8, VW), f32), shape_of((D, 3 * D), bf16)]
        out_shape += [shape_of((2,) * nb + (strip, 2 * v.shape[1]), bf16) for v in shards]
        scratch += [
            pltpu.VMEM((2, 8, VW), f32),
            pltpu.VMEM((2,) * nb + (strip, 3 * D), bf16),
            pltpu.VMEM((HEADS, WIN, WIN), f32),
            pltpu.VMEM((strip, QW), bf16),
            pltpu.VMEM((HEADS, 2 * WT, UP), f32),
            *TABLE_SCRATCH,
            *dma(copies, copies, 1, more, more, len(shards)),
        ]
    out = pl.pallas_call(
        functools.partial(attend_kernel, nb),
        grid=(nw, HEADS // GRP),
        in_specs=[
            kept((nw, WIN)), kept((nw, WIN)), tok, *(kept(v.shape) for v in weights), *[ANY] * len(shards),
        ],
        out_specs=out_specs,
        out_shape=out_shape,
        scratch_shapes=scratch,
        compiler_params=comm_params(2) if nb else PARAMS,
        name="attend",
    )(order, region, x, *weights, *shards)
    if nb:
        return out[:9], [v.reshape(D, v.shape[-1]) for v in out[9:]]
    return (*out, weights[0], weights[1]), []


def run_feed(nw, order, vecs, xc, att, cot, wo, we, wr):
    rows = nw * WIN
    tok = per((WIN, D))
    return pl.pallas_call(
        feed_kernel,
        grid=(nw,),
        in_specs=[
            kept((nw, WIN)), kept((2, 8, VW)), tok, tok, tok, kept((D, D)), kept((D, FF)), kept((D, FF)),
        ],
        out_specs=[
            tok, tok, whole((2, D, FF // 2)), whole((2, D, FF // 2)), whole((2, D, HALF)), whole((8, D)),
        ],
        out_shape=[
            shape_of((rows, D), bf16),
            shape_of((rows, D), f32),
            shape_of((2, D, FF // 2), bf16),
            shape_of((2, D, FF // 2), bf16),
            shape_of((2, D, HALF), bf16),
            shape_of((8, D), f32),
        ],
        scratch_shapes=[
            pltpu.VMEM((WIN, D), f32),
            pltpu.VMEM((WIN, D), bf16),
            pltpu.VMEM((WIN, D), bf16),
            pltpu.VMEM((D, WIN), bf16),
            pltpu.VMEM((D, WIN), bf16),
            pltpu.VMEM((WIN, D), f32),
            pltpu.VMEM((WIN, D), f32),
            pltpu.VMEM((D, FF), f32),
            pltpu.VMEM((D, FF), f32),
            pltpu.VMEM((D, D), f32),
            pltpu.VMEM((2, WIN, FC), f32),
            pltpu.VMEM((2, WIN, FC), f32),
            pltpu.VMEM((WIN, FF), bf16),
            pltpu.VMEM((WIN, FF), bf16),
        ],
        compiler_params=PARAMS,
        name="feed",
    )(order, vecs, xc, att, cot, wo, we, wr)


def run_back(nw, nb, order, vecs, xc, nrm, qkv, e, linv, att, mg, w, wo, feed, peak, grads):
    rows = nw * WIN
    tok = per((WIN, D))
    folded = (HEADS, 2 * WT, UP)
    half = (HEADS // 2, 2 * WT, UP)
    scratch = [
        pltpu.VMEM((D, 3 * D), f32),
        pltpu.VMEM((WW, HEADS * WT, WIDE_PAD), bf16),
        pltpu.VMEM((WIN, D), bf16),
        pltpu.VMEM((WIN, D), bf16),
        pltpu.VMEM((D, WIN), bf16),
        pltpu.VMEM((D, WIN), bf16),
        pltpu.VMEM((WIN, D), bf16),
        pltpu.VMEM((2, WIN, WIN), f32),
        pltpu.VMEM((2, WIN, WIN), bf16),
        pltpu.VMEM((WIN, 3 * D), bf16),
        pltpu.VMEM((D, WIN), bf16),
        pltpu.VMEM((D, WIN), bf16),
        pltpu.VMEM((HEADS, WIN, WIN), f32),
        pltpu.VMEM((HEADS * WT, WIDE_PAD), f32),
        pltpu.VMEM((WIN, D), f32),
    ]
    out_specs = [tok, whole((VEC_ROWS, D))]
    out_shape = [shape_of((rows, D), bf16), shape_of((VEC_ROWS, D), f32)]
    plans = []
    if nb:
        strip = D >> nb
        widths = [v.shape[2] for v in grads]
        plans = [stream_plan(nb, widths, strip), stream_plan(nb, [QW], strip)]
        copies = [len(plan) * (nb + 1) for plan in plans]
        more = copies[1] + 2 * (nb + 1)
        out_specs += [whole(half), whole((strip, QW)), *(whole((strip, width)) for width in widths)]
        out_shape += [shape_of(half, f32), shape_of((strip, QW), f32)]
        out_shape += [shape_of((strip, width), f32) for width in widths]
        scratch += [
            pltpu.VMEM((2,) * (nb + 1) + (strip, QW), bf16),
            pltpu.VMEM(folded, f32),
            pltpu.VMEM((strip, QW), f32),
            pltpu.VMEM((nb + 1, VEC_ROWS, D), f32),
            pltpu.VMEM((nb + 1, VEC_ROWS, D), f32),
            pltpu.VMEM((nb + 2, *half), bf16),
            pltpu.VMEM((nb + 1, *half), bf16),
        ]
        for plan, among in zip(plans, (widths, [QW])):
            for m, first, size, order_of in plan:
                scratch += Scatter.arrivals(nb, size, among[m])
        scratch += dma(copies[0], copies[0], len(plans[0]), more, more, len(plans[1]))
        grads = [v.reshape((2,) * (nb + 1) + (strip, v.shape[2])) for v in grads]
    else:
        grads = []
        out_specs += [whole(folded), whole((2, D, QW))]
        out_shape += [shape_of(folded, f32), shape_of((2, D, QW), bf16)]
    return pl.pallas_call(
        functools.partial(back_kernel, nb, plans),
        grid=(nw, HEADS // GRP),
        in_specs=[
            kept((nw, WIN)), kept((2, 8, VW)), tok, tok, per((WIN, 3 * D)), EXPS, tok, tok, tok,
            kept((D, 3 * D)), kept((D, D)), kept((8, D)), kept((8, D)), *[ANY] * len(grads),
        ],
        out_specs=out_specs,
        out_shape=out_shape,
        scratch_shapes=scratch,
        compiler_params=comm_params(3) if nb else PARAMS,
        name="attend_back",
    )(order, vecs, xc, nrm, qkv, e, linv, att, mg, w, wo, feed, peak, *grads)


BOTH = ("wide", "tensor")
MESH = pl.DeviceIdType.MESH


def bits_of(groups):
    return groups.bit_length() - 1


def orders_of(nb):
    down = tuple(reversed(range(nb)))
    return (down, down[:-2] + (down[-1], down[-2])) if nb > 1 else (down, down)


class Place:
    def __init__(self, nb):
        self.nb = nb
        self.w = lax.axis_index("wide")
        self.t = lax.axis_index("tensor")
        self.bit = [self.w // (1 << k) % 2 for k in range(nb)]

    def across(self, k):
        return (self.w + (1 - 2 * self.bit[k]) * (1 << k), self.t)

    def sibling(self):
        return (self.w, 1 - self.t)

    def greet(self):
        barrier = pltpu.get_barrier_semaphore()
        partners = [self.across(k) for k in range(self.nb)] + [self.sibling()]
        for partner in partners:
            pl.semaphore_signal(barrier, inc=1, device_id=partner, device_id_type=MESH)
        pl.semaphore_wait(barrier, len(partners))

    def index(self, chosen):
        return tuple(chosen.get(k, slice(None)) for k in reversed(range(self.nb)))


def remote(src, dst, send, recv, to):
    return pltpu.make_async_remote_copy(
        src_ref=src, dst_ref=dst, send_sem=send, recv_sem=recv, device_id=to, device_id_type=MESH
    )


class Gather:
    def __init__(self, place, owns, bufs, send, recv, near):
        self.place, self.owns, self.bufs = place, owns, bufs
        self.send, self.recv, self.near = send, recv, near
        nb = place.nb
        self.streams = []
        for own, buf in zip(owns, bufs):
            strip = own.shape[0]
            for half, order in enumerate(orders_of(nb)):
                self.streams.append((own, buf, pl.ds(half * strip // 2, strip // 2), order))

    @staticmethod
    def copies(nb, count):
        return count * (2 * nb + 1)

    def lanes(self, own):
        width = own.shape[1]
        return pl.ds(pl.multiple_of(self.place.t * width, 128), width)

    def local(self, b):
        own, buf = self.owns[b], self.bufs[b]
        mine = self.place.index(dict(enumerate(self.place.bit)))
        return pltpu.make_async_copy(own, buf.at[(*mine, slice(None), self.lanes(own))], self.near.at[b])

    def wide(self, s, p):
        own, buf, rows, order = self.streams[s]
        place = self.place
        chosen = {k: place.bit[k] for k in order[p:]}
        region = buf.at[(*place.index(chosen), rows, self.lanes(own))]
        src = region if p else own.at[rows, :]
        at = s * place.nb + p
        return remote(src, region, self.send.at[at], self.recv.at[at], place.across(order[p]))

    def core(self, b):
        own, buf = self.owns[b], self.bufs[b]
        region = buf.at[(*self.place.index({}), slice(None), self.lanes(own))]
        at = len(self.streams) * self.place.nb + b
        return remote(region, region, self.send.at[at], self.recv.at[at], self.place.sibling())

    def step(self, p):
        nb = self.place.nb
        streams, count = range(len(self.streams)), range(len(self.bufs))
        if p == 0:
            for b in count:
                self.local(b).start()
        elif p == 1:
            for b in count:
                self.local(b).wait()
        if 0 < p <= nb:
            for s in streams:
                self.wide(s, p - 1).wait_recv()
        if p < nb:
            for s in streams:
                self.wide(s, p).start()
        elif p == nb:
            for b in count:
                self.core(b).start()
        else:
            for s in streams:
                for q in range(nb):
                    self.wide(s, q).wait_send()
            for b in count:
                self.core(b).wait()

    def steps(self):
        return self.place.nb + 2


class Scatter:
    def __init__(self, place, streams, send, recv, near):
        self.place, self.streams = place, streams
        self.send, self.recv, self.near = send, recv, near

    @staticmethod
    def arrivals(nb, rows, width):
        return [pltpu.VMEM((2,) * (nb - max(p, 0)) + (rows, width), bf16) for p in range(-1, nb + 1)]

    def local(self, s):
        matrix, first, size, order, (own, *arrive), out = self.streams[s]
        src = matrix.at[(self.place.t, *self.place.index({}), pl.ds(first, size), slice(None))]
        return pltpu.make_async_copy(src, own, self.near.at[s])

    def left(self, order, p):
        return [k for k in reversed(range(self.place.nb)) if k not in order[:p]]

    def copy(self, s, p):
        matrix, first, size, order, (own, *arrive), out = self.streams[s]
        place = self.place
        if p == 0:
            src, to = matrix.at[(1 - place.t, *place.index({}), pl.ds(first, size), slice(None))], place.sibling()
        else:
            k = order[p - 1]
            src = arrive[p - 1].at[self.part(order, p, 1 - place.bit[k])]
            to = place.across(k)
        at = s * (place.nb + 1) + p
        return remote(src, arrive[p], self.send.at[at], self.recv.at[at], to)

    def part(self, order, p, value):
        return tuple(value if k == order[p - 1] else slice(None) for k in self.left(order, p - 1))

    def add(self, s, p):
        matrix, first, size, order, (own, *arrive), out = self.streams[s]
        place = self.place
        left = self.left(order, p)

        def one(i, carry):
            picked = {k: i // (1 << j) % 2 for j, k in enumerate(left)}
            there = (*(picked[k] for k in left), slice(None), slice(None))
            if p == 0:
                here = own[there]
            else:
                picked[order[p - 1]] = place.bit[order[p - 1]]
                before = tuple(picked[k] for k in self.left(order, p - 1))
                here = arrive[p - 1][(*before, slice(None), slice(None))]
            total = here.astype(f32) + arrive[p][there].astype(f32)
            if left:
                arrive[p][there] = total.astype(bf16)
            else:
                out[first : first + size, :] = total
            return carry

        if left:
            lax.fori_loop(0, 1 << len(left), one, 0)
        else:
            one(0, 0)

    def step(self, p):
        nb = self.place.nb
        for s in range(len(self.streams)):
            if p == 0:
                self.local(s).start()
            if p == 1:
                self.local(s).wait()
            if p:
                self.copy(s, p - 1).wait_recv()
                self.add(s, p - 1)
            if p <= nb:
                self.copy(s, p).start()
        if p == nb + 1:
            for s in range(len(self.streams)):
                for q in range(nb + 1):
                    self.copy(s, q).wait_send()

    def steps(self):
        return self.place.nb + 2


GATHER_TIMES = (0.0, 0.07, 0.25, 0.44, 0.75, 0.94)
SCATTER_TIMES = (0.0, 0.13, 0.5, 0.7, 0.88, 1.0)


def run_beside(transfer, at_step, times):
    total = pl.num_programs(0) * pl.num_programs(1)
    for p in range(1, transfer.steps()):
        when = times[min(p, len(times) - 1)]
        if when < 1.0:

            @pl.when(at_step == int(when * 64) * total // 64)
            def _():
                transfer.step(p)


def comm_params(collective_id, **more):
    return pltpu.CompilerParams(
        vmem_limit_bytes=VMEM_LIMIT, collective_id=collective_id, has_side_effects=True, **more
    )


def stream_plan(nb, widths, strip):
    first, second = (tuple(reversed(order)) for order in orders_of(nb))
    plan = []
    for m in range(len(widths)):
        plan.append((m, 0, strip // 2, first))
        plan.append((m, strip // 2, strip // 2, second))
    return plan


def build_streams(plan, matrices, arrive, outs, nb):
    streams = []
    for i, (m, first, size, order) in enumerate(plan):
        streams.append((matrices[m], first, size, order, arrive[i * (nb + 2) : (i + 1) * (nb + 2)], outs[m]))
    return streams


class Sums:
    def __init__(self, place, vec, vec_in, table, table_in, send, recv, base):
        self.place, self.base = place, base
        self.vec, self.vec_in, self.table, self.table_in = vec, vec_in, table, table_in
        self.send, self.recv = send, recv

    def pair(self, p):
        place = self.place
        to = place.across(p - 1) if p else place.sibling()
        at = self.base + 2 * p
        table = self.table.at[1 - place.t] if p == 0 else self.table.at[p + 1]
        return (
            remote(self.vec.at[p], self.vec_in.at[p], self.send.at[at], self.recv.at[at], to),
            remote(table, self.table_in.at[p], self.send.at[at + 1], self.recv.at[at + 1], to),
        )

    def step(self, p, vec_out, table_out):
        nb = self.place.nb
        if p:
            vec, table = self.pair(p - 1)
            vec.wait_recv()
            table.wait_recv()
            mine, theirs = self.vec[p - 1], self.vec_in[p - 1]
            summed = iota(mine.shape, 0) < SUM_ROWS
            total = jnp.where(summed, mine + theirs, jnp.maximum(mine, theirs))
            mine = self.table[self.place.t] if p == 1 else self.table[p]
            table_total = mine.astype(f32) + self.table_in[p - 1].astype(f32)
            if p <= nb:
                self.vec[p] = total
                self.table[p + 1] = table_total.astype(bf16)
            else:
                vec_out[...] = total
                table_out[...] = table_total
        if p <= nb:
            for copy in self.pair(p):
                copy.start()
        else:
            for q in range(nb + 1):
                for copy in self.pair(q):
                    copy.wait_send()


def body(
    inputs, cotangent, window_order, region_ids, clip_threshold, norm1_gain, norm1_shift,
    qkv_weight, qv_bias, rel_table, out_weight, out_bias, norm2_gain, norm2_shift,
    expand_weight, expand_bias, reduce_weight, reduce_bias,
):
    parts = lax.axis_size("tensor")
    groups = lax.axis_size("wide")
    mine = lax.axis_index("tensor")
    own = HEADS // parts
    oc, fc = D // parts, FF // parts
    nw = inputs.shape[0] // WIN
    strip = D // groups
    nb = bits_of(groups)
    paired = parts == 2 and groups == 1 << nb and nb > 0 and strip % 32 == 0

    order = lax.dynamic_slice_in_dim(window_order, mine * nw, nw, 0)
    region = lax.dynamic_slice_in_dim(region_ids, mine * nw * WIN, nw * WIN, 0)
    region = region.reshape(nw, WIN).astype(f32)

    def params(first):
        rows = [norm1_gain, norm1_shift, norm2_gain, norm2_shift, out_bias, reduce_bias]
        rows = jnp.pad(jnp.stack(rows + [jnp.zeros((D,), bf16)]), ((0, 0), (0, VW - D)))
        return jnp.concatenate([first[None], rows], axis=0).astype(f32)

    if paired:
        first = jnp.concatenate([qv_bias[0], jnp.zeros((oc,), bf16), qv_bias[1], expand_bias])
        weights = [params(first), padded_table(rel_table), qkv_weight]
        shards = [out_weight.T, expand_weight, reduce_weight.T]
    else:
        qkv_strip = qkv_weight.reshape(strip, own, 3, HD).transpose(0, 2, 1, 3).reshape(strip, 3 * oc)
        shard = jnp.concatenate([qkv_strip, out_weight.T, expand_weight, reduce_weight.T], axis=1)
        full = lax.all_gather(shard, BOTH, axis=0)
        full = full.reshape(groups, parts, strip, shard.shape[1]).transpose(0, 2, 1, 3)
        full = full.reshape(D, parts, shard.shape[1])
        wqkv = full[:, :, : 3 * oc].reshape(D, parts, 3, oc).transpose(0, 2, 1, 3)
        wqkv = wqkv.reshape(D, 3, 2, HALF).transpose(0, 2, 1, 3).reshape(D, 3 * D)
        wo = full[:, :, 3 * oc : 4 * oc].reshape(D, D)
        we = full[:, :, 4 * oc : 4 * oc + fc].reshape(D, FF)
        wr = full[:, :, 4 * oc + fc :].reshape(D, FF)
        small = jnp.concatenate([qv_bias.reshape(-1), expand_bias, rel_table.reshape(-1)])
        small = lax.all_gather(small, "tensor", axis=0)
        qv = small[:, : 2 * oc].reshape(parts, 2, oc).transpose(1, 0, 2).reshape(2, 2, HALF)
        be = small[:, 2 * oc : 2 * oc + fc].reshape(2, FF // 2)
        zero = jnp.zeros((HALF,), bf16)
        vecs = jnp.stack([params(jnp.concatenate([qv[0, v], zero, qv[1, v], be[v]])) for v in range(2)])
        weights = [vecs, wqkv, table_bias(small[:, 2 * oc + fc :].reshape(HEADS, RT))]
        shards = []
        nb = 0

    (xc, nrm, qkv, e, linv, att, peak, vecs, wqkv), gathered = run_attend(
        nw, nb, order, region, inputs, weights, shards
    )
    if paired:
        wo, we, wr = gathered
    layer_out, mg, gwe, gwr, gwo, feed = run_feed(nw, order, vecs, xc, att, cotangent, wo, we, wr)
    input_grad, sums, table, qkv_own, *summed = run_back(
        nw, nb, order, vecs, xc, nrm, qkv, e, linv, att, mg, wqkv, wo, feed, peak, [gwo, gwe, gwr]
    )
    if paired:
        out_own, expand_own, reduce_own = summed
        qkv_out = qkv_own
    else:
        gw = qkv_own

        def cut(grad, width):
            return grad.transpose(1, 0, 2).reshape(D, parts, width).astype(f32)

        gw = gw.reshape(2, D, 3, HALF).transpose(1, 2, 0, 3).reshape(D, 3, parts, oc)
        gw = gw.transpose(0, 2, 1, 3).reshape(D, parts, 3 * oc).astype(f32)
        grads = jnp.concatenate([gw, cut(gwo, oc), cut(gwe, fc), cut(gwr, fc)], axis=2)
        grads = grads.reshape(groups, strip, parts, 4 * oc + 2 * fc).transpose(0, 2, 1, 3)
        grads = grads.reshape(groups * parts * strip, 4 * oc + 2 * fc)
        grads = lax.psum_scatter(grads, BOTH, scatter_dimension=0, tiled=True)
        qkv_out = grads[:, : 3 * oc].reshape(strip, 3, own, HD).transpose(0, 2, 1, 3).reshape(strip, 3 * oc)
        out_own = grads[:, 3 * oc : 4 * oc]
        expand_own, reduce_own = grads[:, 4 * oc : 4 * oc + fc], grads[:, 4 * oc + fc :]
        table = lax.dynamic_slice_in_dim(lax.psum(table, BOTH), mine * own, own, 0)
        sums = jnp.concatenate(
            [lax.psum(sums[:SUM_ROWS], BOTH), lax.pmax(sums[SUM_ROWS:], BOTH)], axis=0
        )

    table_own = table[:, : 2 * WT - 1, :ROWS].reshape(own, RT)
    dbe_own = lax.dynamic_slice_in_dim(sums[6:10].reshape(FF), mine * fc, fc, 0)
    heads_grad = sums[10:13].reshape(2, 3, HALF)
    bias_grad = jnp.stack([heads_grad[:, 0].reshape(D), heads_grad[:, 2].reshape(D)], axis=0)
    bias_own = lax.dynamic_slice_in_dim(bias_grad, mine * oc, oc, 1)
    peak_own = lax.dynamic_slice_in_dim(sums[SUM_ROWS], mine * own, own, 0)
    factor = jnp.sqrt(clip_threshold / jnp.maximum(peak_own, clip_threshold))
    column_factor = jnp.stack([factor, factor, jnp.ones_like(factor)], axis=1)
    clipped_qkv = (
        qkv_weight.astype(f32).reshape(strip, own, 3, HD) * column_factor[None, :, :, None]
    ).reshape(qkv_weight.shape)
    bias_scale = jnp.stack([jnp.repeat(factor, HD), jnp.ones((own * HD,), f32)], axis=0)
    clipped_bias = qv_bias.astype(f32) * bias_scale
    return (
        layer_out,
        input_grad,
        sums[0],
        sums[1],
        qkv_out,
        bias_own,
        table_own,
        out_own.T,
        sums[5],
        sums[2],
        sums[3],
        expand_own,
        dbe_own,
        reduce_own.T,
        sums[4],
        peak_own,
        clipped_qkv,
        clipped_bias,
    )


def solution(mesh):
    tokens = P(BOTH, None)
    in_specs = (
        tokens, tokens, P("wide", None), P("wide"), P(), P(), P(), P("wide", "tensor"),
        P(None, "tensor"), P("tensor", None), P("tensor", "wide"), P(), P(), P(),
        P("wide", "tensor"), P("tensor"), P("tensor", "wide"), P(),
    )
    out_specs = (
        tokens, tokens, P(), P(), P("wide", "tensor"), P(None, "tensor"), P("tensor", None),
        P("tensor", "wide"), P(), P(), P(), P("wide", "tensor"), P("tensor"),
        P("tensor", "wide"), P(), P("tensor"), P("wide", "tensor"), P(None, "tensor"),
    )
    return jax.shard_map(body, mesh=mesh, in_specs=in_specs, out_specs=out_specs, check_vma=False)
```

time: 671 us -> 225 us (0.34); the launches traced: 661 us -> 224 us
  waiting for transfers between devices: 219 us -> 0 us
  local copies, waits for them, and re-layouts: 119 us -> 19 us
  blocking collectives: 79.6 us -> 0 us
  other arithmetic: 22.7 us -> 4.84 us
  between operations: 18 us -> 1.4 us
    reduce_scatter x1 -> x0, waiting for transfers between devices: 161 us -> none  [body(): mine_grad = lax.psum_scatter(grads, BOTH, scatter_dimension=0, tiled=True)]
    reshape x19 -> x3, local copies, waits for them, and re-layouts: 56.8 us -> 2.64 us  [the longest x1 1.66 us: body(): table_own = table[:, :2 * WT - 1, :ROWS].reshape(own, RT)]
    psum x1 -> x0, blocking collectives: 40.3 us -> none  [body(): sums = lax.psum((vec1[:2], vec2[:4], dbe, bias_grad, table_grad), BOTH)]
    pmax x1 -> x0, blocking collectives: 39.3 us -> none  [body(): peak = lax.pmax(jnp.max(hm, axis=(1, 2)) * SCALE, BOTH)]
    psum x1 -> x0, waiting for transfers between devices: 25.8 us -> none  [body(): sums = lax.psum((vec1[:2], vec2[:4], dbe, bias_grad, table_grad), BOTH)]
    all_gather x1 -> x0, waiting for transfers between devices: 22.4 us -> none  [body(): full = lax.all_gather(shard, BOTH, axis=0)]
    concatenate x5 -> x0, local copies, waits for them, and re-layouts: 16.9 us -> none  [the longest x4 16.8 us: body(): jnp.concatenate([dw.reshape(D, 3, parts, oc).transpose(2, 0, 1, 3).reshap...]
    concatenate x5 -> x1, other arithmetic: 11.5 us -> 0.69 us  [body(): jnp.concatenate([qv_bias[0], jnp.zeros((oc,), bf16), qv_bias[1], expand_b...]
  transfers between devices with their start and end apart: 4 -> 0, of which waited for: 4 -> 0; matrix products, arithmetic and copies ran while one was open for 7% -> 0% of each run, Pallas kernels for 2% -> 0%
where the time goes in v2:
time: 225 us; the launch traced here: 224 us
  Pallas kernels  199 us (88%)
  local copies, waits for them, and re-layouts  19 us (8%)
  other arithmetic  4.84 us (2%)
    pallas_call x1, Pallas kernels, run_back(): pl.pallas_call(functools.partial(back_kernel, nb, plans), grid=(nw, HEADS...  85.8 us
    pallas_call x1, Pallas kernels, run_attend(): pl.pallas_call(functools.partial(attend_kernel, nb), grid=(nw, HEADS // G...  71.1 us
    pallas_call x1, Pallas kernels, run_feed(): pl.pallas_call(feed_kernel, grid=(nw,), in_specs=[kept((nw, WIN)), kept((...  42.1 us
    unnamed x21, local copies, waits for them, and re-layouts  6.8 us

profile of v2, /device:TPU:0, one launch (start us, length us, event | category | flops | bytes accessed | tf_op | source)
XLA Modules:
  0.0 224.3 jit_solution(16044973541419416668)
XLA Ops:
  0.7 0.0 copy-start
  0.7 0.7 copy-done
  1.4 0.6 constant_dynamic-slice_fusion.1.order_ref
  2.0 0.8 dynamic-slice_convert_fusion
  2.8 0.7 convert_element_type.20.region_ref
  3.4 0.8 slice_reduce_fusion.1
  4.2 0.7 pad_maximum_fusion
  4.9 0.7 stack.32
  5.6 0.7 stack.33
  6.3 0.7 stack.34
  7.0 0.7 stack.35
  7.7 0.7 stack.36
  8.3 0.7 stack.37
  9.1 0.6 fusion.2.rest_0_
  9.7 1.0 reshape.95
  10.7 0.7 pad_convert_fusion.rest_1_
  11.3 71.1 %attend.1 = (bf16[1568,512]{1,0:T(8,128)(2,1)}, bf16[1568,512]{1,0:T(8,128)(2,1)}, bf16[1568,1536]{1,0:T(8,128)(2,1)}, bf16[4,16,392,392]{3,2,1,0:T(8,128)(2,1)}...) custom-call(s32[4,392]{1,0:T(4,128)} %constant_dynamic-slice_fusion., ...), custom_call_target="tpu_custom_call" | custom-call | tf_op jit(solution)/shard_map/attend/pallas_call | solution.py:661
  82.5 42.1 %feed.1 = (bf16[1568,512]{1,0:T(8,128)(2,1)}, f32[1568,512]{1,0:T(8,128)}, bf16[2,512,1024]{2,1,0:T(8,128)(2,1)}, bf16[2,512,1024]{2,1,0:T(8,128)(2,1)}, bf16[2,512,256]{2,1,0:T(8,128)(2,1)}, /*index=5*/f32[8,512]{1,0:T(8,128)}) custom-call(s32[4,392]{1,0:T(4,128)} %constant_dynamic-slice_fusion.1.order_ref, f32[2,8,1792]{2,1,0:T(8,128)} %get-tuple-element.43.vecs_ref, ...), custom_call_target="tpu_custom_call" | custom-call | tf_op jit(solution)/shard_map/feed/pallas_call | solution.py:681
  124.6 0.0 copy-start.6
  124.6 0.0 copy-start.1
  124.6 85.8 %attend_back.1 = (bf16[1568,512]{1,0:T(8,128)(2,1)}, f32[24,512]{1,0:T(8,128)}, f32[8,16,256]{2,1,0:T(8,128)}, f32[32,768]{1,0:T(8,128)}, f32[32,256]{1,0:T(8,12...) custom-call(s32[4,392]{1,0:T(4,128)} %constant_dynamic-slice_fusion.1.order_ref, f32[2,8,1792]{2,1,0:T(8,128)} %get-tuple-element.43.vecs_ref, ...), custom_call_target="tpu_custom_call" | custom-call | tf_op jit(solution)/shard_map/attend_back/pallas_call | solution.py:771
  210.4 1.5 fusion.6
  212.6 0.6 divide_sqrt_fusion
  213.2 0.1 broadcast_in_dim.12
  213.3 0.1 stack_reshape.3
  213.4 0.7 slice.46
  214.1 0.0 copy-done.6
  214.1 0.7 fusion.3
  214.8 0.1 sqrt_bitcast_fusion
  214.9 0.1 pad.16.clone
  215.0 0.1 maximum_maximum_fusion
  215.0 0.1 copy.37
  215.1 0.1 mul.37
  215.2 0.1 mul.38
  215.3 0.0 copy-done.1
  215.3 0.7 convert_multiply_fusion
  215.9 1.7 reshape.103
  217.6 0.8 slice_bitcast_fusion
  218.4 0.6 dynamic_slice.20
  219.0 2.7 %copy.45 = bf16[1568,512]{1,0:T(8,128)(2,1)} copy(bf16[1568,512]{1,0:T(8,128)(2,1)} %get-tuple-element.102) | data formatting | bytes 3211264
  221.7 0.0 copy-done.4
  221.7 0.6 copy.46
  222.3 0.0 copy-done.5
  222.3 0.6 copy.47
  223.0 0.0 copy-done.3
  223.0 0.7 copy.48
  223.6 0.0 copy-done.2
  223.6 0.7 copy.49
  (11 shorter events, 0.1 us)
Async XLA Ops:
  0.7 0.7 copy-start
  124.6 89.5 %copy-start.6 = (bf16[2,256]{1,0:T(2,128)(2,1)S(1)}, bf16[2,256]{1,0:T(2,128)(2,1)}, u32[]{:S(2)}) copy-start(bf16[2,256]{1,0:T(2,128)(2,1)} %param.26) | copy-start | bytes 3076
  124.6 90.7 %copy-start.1 = (bf16[32,768]{1,0:T(8,128)(2,1)S(1)}, bf16[32,768]{1,0:T(8,128)(2,1)}, u32[]{:S(2)}) copy-start(bf16[32,768]{1,0:T(8,128)(2,1)} %rest_2_.1) | copy-start | bytes 147460
  219.0 2.7 %copy-start.4 = (f32[32,768]{1,0:T(8,128)S(1)}, f32[32,768]{1,0:T(8,128)}, u32[]{:S(2)}) copy-start(f32[32,768]{1,0:T(8,128)} %get-tuple-element.105) | copy-start | bytes 294916
  219.0 3.4 %copy-start.5 = (f32[32,256]{1,0:T(8,128)S(1)}, f32[32,256]{1,0:T(8,128)}, u32[]{:S(2)}) copy-start(f32[32,256]{1,0:T(8,128)} %get-tuple-element.65) | copy-start | bytes 98308
  219.0 4.0 %copy-start.3 = (f32[32,1024]{1,0:T(8,128)S(1)}, f32[32,1024]{1,0:T(8,128)}, u32[]{:S(2)}) copy-start(f32[32,1024]{1,0:T(8,128)} %get-tuple-element.112) | copy-start | bytes 393220
  219.0 4.7 %copy-start.2 = (f32[32,1024]{1,0:T(8,128)S(1)}, f32[32,1024]{1,0:T(8,128)}, u32[]{:S(2)}) copy-start(f32[32,1024]{1,0:T(8,128)} %get-tuple-element.67) | copy-start | bytes 393220

commit v3 on v2

--- a/solution.py
+++ b/solution.py
@@ -3,6 +3,7 @@
 
 import jax
 import jax.numpy as jnp
+import numpy as np
 from jax import lax
 from jax.experimental import pallas as pl
 from jax.experimental.pallas import tpu as pltpu
@@ -41,7 +42,7 @@
 NT = (((1,), (1,)), ((), ()))
 TN = (((0,), (0,)), ((), ()))
 
-VMEM_LIMIT = 60 * 2**20
+VMEM_LIMIT = 62 * 2**20
 
 
 def dot(a, b, dims=NN):
@@ -106,6 +107,14 @@
     return (iota((FLAT_PAD, WIDE_PAD), 0) == target).astype(f32).astype(bf16)
 
 
+def spread_constant():
+    column = np.arange(WIDE_PAD)
+    rest = column % (WW * WT)
+    target = rest % WT * PITCH + (12 - column // (WW * WT)) * 13 + 6 - rest // WT
+    target = np.where(column < WIDE_SEG, target, -1)
+    return jnp.asarray(np.arange(FLAT_PAD)[:, None] == target[None, :], bf16)
+
+
 def flatten_table(table_ref, flat_ref):
     total = None
     rest = jnp.zeros((HEADS * WT, FLAT_PAD - UP), f32)
@@ -162,7 +171,7 @@
     )(padded_table(table))
 
 
-def fold_table(table_scr, seg_scr, wide_scr, out_ref):
+def fold_table(table_scr, seg_scr, wide_scr, spread_ref, out_ref):
     seg_scr[...] = jnp.zeros_like(seg_scr)
     for wi in range(WW):
         total = None
@@ -175,7 +184,7 @@
                 moved = pltpu.roll(moved, off, 1)
             total = moved if total is None else total + moved
         wide_scr[wi] = total.astype(bf16)
-    flat = dot(wide_scr[...].reshape(WW * HEADS * WT, WIDE_PAD), one_hot_spread(), NT)
+    flat = dot(wide_scr[...].reshape(WW * HEADS * WT, WIDE_PAD), spread_ref[...], NT)
     total = None
     for wi in range(WW):
         part = flat[wi * HEADS * WT : (wi + 1) * HEADS * WT, :]
@@ -187,7 +196,7 @@
         out_ref[:, WT - 1 - tj : 2 * WT - 1 - tj, :] += rows[:, :UP].reshape(HEADS, WT, UP)
 
 
-def attend_kernel(nb, order_ref, region_ref, x_ref, *rest):
+def attend_kernel(nw, nb, order_ref, region_ref, x_ref, *rest):
     if nb:
         (params_ref, table_ref, own_ref), shards, rest = rest[:3], rest[3:6], rest[6:]
     else:
@@ -195,7 +204,7 @@
     (xc_ref, nrm_ref, qkv_ref, e_ref, linv_ref, att_ref, peak_ref), rest = rest[:7], rest[7:]
     if nb:
         (vecs_out, w_out), bufs, rest = rest[:2], rest[2:5], rest[5:]
-    (x_scr, mask_scr, hm_ref), rest = rest[:3], rest[3:]
+    (x_scr, mask_scr, hm_ref, xc_scr, nrm_scr), rest = rest[:5], rest[5:]
     w, g = pl.program_id(0), pl.program_id(1)
     at_step = w * (HEADS // GRP) + g
     opening = (w == 0) & (g == 0)
@@ -203,7 +212,8 @@
         (vecs_ref, w_scr, bias_ref, own_scr, tables, flat_ref, wide_ref, turned_ref), sems = rest[:8], rest[8:]
         place = Place(nb)
         first = Gather(place, [own_scr], [w_scr], *sems[:3])
-        second = Gather(place, shards, bufs, *sems[3:])
+        second = Gather(place, shards[:1], bufs[:1], *sems[3:6])
+        third = Gather(place, shards[1:], bufs[1:], *sems[6:])
         base = Gather.copies(nb, 1)
         mine = pl.ds(pl.multiple_of(place.t * (HEADS // 2), HEADS // 2), HEADS // 2)
         near = [
@@ -211,19 +221,23 @@
             for i, part in enumerate((tables.at[mine], vecs_ref.at[place.t]))
         ]
 
-    def prepare():
-        pick = picks_of(order_ref, w)
-        region = region_ref[pl.ds(w, 1), :]
+    def prepare(i):
+        pick = picks_of(order_ref, i)
+        region = region_ref[pl.ds(i, 1), :]
         row_at = jnp.sum(jnp.where(pick, region, 0.0), axis=1, keepdims=True)
         pick = one_hot(pick)
         column_at = dot(jnp.broadcast_to(region, (8, WIN)).astype(bf16), pick, NT)[0:1, :]
-        mask_scr[...] = jnp.where(row_at == column_at, 0.0, masked * LOG2E)
-        xc_ref[...] = dot(pick, x_ref[...]).astype(bf16)
+        mask_scr[i] = jnp.where(row_at == column_at, 0.0, masked * LOG2E)
+        xc_scr[i] = dot(pick, x_ref[i]).astype(bf16)
         for at, size in ROW_CHUNKS:
-            centered, rstd = moments(xc_ref[at : at + size, :].astype(f32))
-            nrm_ref[at : at + size, :] = (centered * rstd * vecs_ref[0, 1:2, 0:D] + vecs_ref[0, 2:3, 0:D]).astype(bf16)
+            centered, rstd = moments(xc_scr[i, at : at + size, :].astype(f32))
+            nrm_scr[i, at : at + size, :] = (
+                centered * rstd * vecs_ref[0, 1:2, 0:D] + vecs_ref[0, 2:3, 0:D]
+            ).astype(bf16)
 
     def project():
+        xc_ref[...] = xc_scr[w]
+        nrm_ref[...] = nrm_scr[w]
         weight = w_scr[...].reshape(D, 3 * D) if nb else w_ref
         for v in range(2):
             cols = slice(v * QW, (v + 1) * QW)
@@ -246,7 +260,7 @@
             for at, size in ROW_CHUNKS:
                 xx = x_scr[hh % 2, at : at + size, :]
                 top = jnp.maximum(top, jnp.max(xx.reshape(size // 8, 8, WIN), axis=0))
-                s = xx * (SCALE * LOG2E) + bias_ref[h, at : at + size, :] + mask_scr[at : at + size, :]
+                s = xx * (SCALE * LOG2E) + bias_ref[h, at : at + size, :] + mask_scr[w, at : at + size, :]
                 e_ref[0, hh, at : at + size, :] = jnp.exp2(s - jnp.max(s, axis=1, keepdims=True)).astype(bf16)
             hm_ref[h] = top
 
@@ -274,6 +288,13 @@
     @pl.when(opening)
     def _():
         hm_ref[...] = jnp.full(hm_ref.shape, lowest, f32)
+        windows = list(range(nw))
+
+        def some(count):
+            for i in windows[:count]:
+                prepare(i)
+            del windows[:count]
+
         if nb:
             place.greet()
             own_scr[...] = dot(own_ref[...], column_moves()).astype(bf16)
@@ -286,26 +307,27 @@
                 copy.wait()
             flatten_table(tables, flat_ref)
             first.step(1)
-
-    @pl.when(g == 0)
-    def _():
-        prepare()
-
-    if nb:
-
-        @pl.when(opening)
-        def _():
+            some(1)
             first.step(2)
+            second.step(0)
             turn_table(flat_ref, wide_ref, turned_ref)
             first.step(3)
-            second.step(0)
+            second.step(1)
             spread_table(turned_ref, bias_ref)
-            for p in range(4, first.steps()):
+            some(1)
+            first.step(4)
+            second.step(2)
+            third.step(0)
+            some(nw)
+            for p in range(5, first.steps()):
                 first.step(p)
             w_out[...] = w_scr[...].reshape(D, 3 * D)
             vecs_out[...] = vecs_ref[...]
-
-        run_beside(second, at_step, GATHER_TIMES)
+        some(nw)
+
+    if nb:
+        run_beside(second, at_step, GATHER_TIMES, 3)
+        run_beside(third, at_step, LATER_TIMES, 1)
 
     @pl.when(g == 0)
     def _():
@@ -432,11 +454,11 @@
 
 def back_kernel(
     nb, plans, order_ref, vecs_ref, xc_ref, nrm_ref, qkv_ref, e_ref, linv_ref, att_ref, mg_ref, w_ref, wo_ref,
-    feed_ref, peak_ref, *rest
+    feed_ref, peak_ref, spread_ref, *rest
 ):
     if nb:
         matrices, rest = rest[:3], rest[3:]
-        (out_ref, sums_out, table_out, qkv_out), outs, rest = rest[:4], rest[4:7], rest[7:]
+        (out_ref, late_out, table_out, qkv_out, early_out), outs, rest = rest[:5], rest[5:8], rest[8:]
     else:
         (out_ref, acc, table_out, gw_ref), rest = rest[:4], rest[4:]
     (
@@ -448,7 +470,7 @@
     at_step = w * (HEADS // GRP) + g
     closing = at_step == pl.num_programs(0) * pl.num_programs(1) - 1
     if nb:
-        (gw_ref, fold_scr, own_out, vec, vec_in, table, table_in), rest = rest[:7], rest[7:]
+        (gw_ref, fold_scr, own_out, vec, vec_in, table, table_in, vec0, vec0_in), rest = rest[:9], rest[9:]
         acc = vec.at[0]
         place = Place(nb)
         count = [len(plan) * (nb + 2) for plan in plans]
@@ -457,6 +479,7 @@
         first = Scatter(place, build_streams(plans[0], matrices, early, outs, nb), *sems[:3])
         second = Scatter(place, build_streams(plans[1], [gw_ref], late, [own_out], nb), *sems[3:])
         sums = Sums(place, vec, vec_in, table, table_in, sems[3], sems[4], len(plans[1]) * (nb + 1))
+        known = Sums(place, vec0, vec0_in, None, None, sems[0], sems[1], len(plans[0]) * (nb + 1))
 
     def prepare():
         ag_scr[...] = mg_ref[...].astype(bf16)
@@ -515,7 +538,7 @@
         for part in range(3):
             cols = slice(part * D, (part + 1) * D)
             dw_ref[:, cols] += dot(nT, pg_scr[:, cols])
-            acc[10 + part : 11 + part, :] += jnp.sum(pg_scr[:, cols].astype(f32), axis=0, keepdims=True)
+            acc[2 + part : 3 + part, :] += jnp.sum(pg_scr[:, cols].astype(f32), axis=0, keepdims=True)
 
     def finish():
         grad_scr[...] = dot(pg_scr[...], w_ref[...], NT)
@@ -536,7 +559,7 @@
     @pl.when(at_step == 0)
     def _():
         dw_ref[...] = jnp.zeros_like(dw_ref)
-        acc[...] = jnp.zeros((VEC_ROWS, D), f32)
+        acc[...] = jnp.zeros((8, D), f32)
         table_scr[...] = jnp.zeros_like(table_scr)
         if nb:
             place.greet()
@@ -544,6 +567,14 @@
 
     if nb:
         run_beside(first, at_step, SCATTER_TIMES)
+        for p in range(nb + 2):
+
+            @pl.when(at_step == pl.num_programs(0) * pl.num_programs(1) * (3 + 2 * p) // (2 * nb + 8))
+            def _():
+                if p == 0:
+                    vec0[0, 0:8, :] = feed_ref[...]
+                    vec0[0, 8:16, :] = peak_ref[...]
+                known.step(p, early_out)
 
     @pl.when(g == 0)
     def _():
@@ -576,21 +607,19 @@
 
     @pl.when(closing)
     def _():
-        acc[2:10, :] = feed_ref[...]
-        acc[SUM_ROWS:VEC_ROWS, :] = peak_ref[...]
         if not nb:
-            fold_table(table_scr, seg_scr, wide_scr, table_out)
+            fold_table(table_scr, seg_scr, wide_scr, spread_ref, table_out)
             return
         second.step(1)
         for p in range(1, first.steps()):
             if SCATTER_TIMES[min(p, len(SCATTER_TIMES) - 1)] >= 1.0:
                 first.step(p)
-        fold_table(table_scr, seg_scr, wide_scr, fold_scr)
+        fold_table(table_scr, seg_scr, wide_scr, spread_ref, fold_scr)
         half = HEADS // 2
         for v in range(2):
             table[v] = fold_scr[v * half : (v + 1) * half].astype(bf16)
         for p in range(second.steps()):
-            sums.step(p, sums_out, table_out)
+            sums.step(p, late_out, table_out)
             if p + 2 < second.steps():
                 second.step(p + 2)
         top = own_out[...].astype(bf16)
@@ -621,8 +650,6 @@
 
 PARAMS = pltpu.CompilerParams(vmem_limit_bytes=VMEM_LIMIT)
 ANY = pl.BlockSpec(memory_space=pl.ANY)
-SUM_ROWS = 16
-VEC_ROWS = 24
 
 
 def dma(*counts):
@@ -642,10 +669,16 @@
         shape_of((rows, D), bf16),
         shape_of((8, D), f32),
     ]
-    scratch = [pltpu.VMEM((2, WIN, WIN), f32), pltpu.VMEM((WIN, WIN), f32), pltpu.VMEM((HEADS, 8, WIN), f32)]
+    scratch = [
+        pltpu.VMEM((2, WIN, WIN), f32),
+        pltpu.VMEM((nw, WIN, WIN), f32),
+        pltpu.VMEM((HEADS, 8, WIN), f32),
+        pltpu.VMEM((nw, WIN, D), bf16),
+        pltpu.VMEM((nw, WIN, D), bf16),
+    ]
     if nb:
         strip = D >> nb
-        copies, more = Gather.copies(nb, 1) + 2, Gather.copies(nb, len(shards))
+        copies, one, more = Gather.copies(nb, 1) + 2, Gather.copies(nb, 1), Gather.copies(nb, len(shards) - 1)
         out_specs += [whole((2, 8, VW)), whole((D, 3 * D)), *[ANY] * len(shards)]
         out_shape += [shape_of((2, 8, VW), f32), shape_of((D, 3 * D), bf16)]
         out_shape += [shape_of((2,) * nb + (strip, 2 * v.shape[1]), bf16) for v in shards]
@@ -656,20 +689,20 @@
             pltpu.VMEM((strip, QW), bf16),
             pltpu.VMEM((HEADS, 2 * WT, UP), f32),
             *TABLE_SCRATCH,
-            *dma(copies, copies, 1, more, more, len(shards)),
+            *dma(copies, copies, 1, one, one, 1, more, more, len(shards) - 1),
         ]
     out = pl.pallas_call(
-        functools.partial(attend_kernel, nb),
+        functools.partial(attend_kernel, nw, nb),
         grid=(nw, HEADS // GRP),
         in_specs=[
-            kept((nw, WIN)), kept((nw, WIN)), tok, *(kept(v.shape) for v in weights), *[ANY] * len(shards),
+            kept((nw, WIN)), kept((nw, WIN)), kept((nw, WIN, D)), *(kept(v.shape) for v in weights), *[ANY] * len(shards),
         ],
         out_specs=out_specs,
         out_shape=out_shape,
         scratch_shapes=scratch,
         compiler_params=comm_params(2) if nb else PARAMS,
         name="attend",
-    )(order, region, x, *weights, *shards)
+    )(order, region, x.reshape(nw, WIN, D), *weights, *shards)
     if nb:
         return out[:9], [v.reshape(D, v.shape[-1]) for v in out[9:]]
     return (*out, weights[0], weights[1]), []
@@ -738,31 +771,34 @@
         pltpu.VMEM((HEADS * WT, WIDE_PAD), f32),
         pltpu.VMEM((WIN, D), f32),
     ]
-    out_specs = [tok, whole((VEC_ROWS, D))]
-    out_shape = [shape_of((rows, D), bf16), shape_of((VEC_ROWS, D), f32)]
+    out_specs = [tok, whole((8, D))]
+    out_shape = [shape_of((rows, D), bf16), shape_of((8, D), f32)]
     plans = []
     if nb:
         strip = D >> nb
         widths = [v.shape[2] for v in grads]
-        plans = [stream_plan(nb, widths, strip), stream_plan(nb, [QW], strip)]
+        plans = [stream_plan(nb, widths), stream_plan(nb, [QW])]
         copies = [len(plan) * (nb + 1) for plan in plans]
         more = copies[1] + 2 * (nb + 1)
-        out_specs += [whole(half), whole((strip, QW)), *(whole((strip, width)) for width in widths)]
-        out_shape += [shape_of(half, f32), shape_of((strip, QW), f32)]
+        out_specs += [whole(half), whole((strip, QW)), whole((16, D))]
+        out_specs += [whole((strip, width)) for width in widths]
+        out_shape += [shape_of(half, f32), shape_of((strip, QW), f32), shape_of((16, D), f32)]
         out_shape += [shape_of((strip, width), f32) for width in widths]
         scratch += [
             pltpu.VMEM((2,) * (nb + 1) + (strip, QW), bf16),
             pltpu.VMEM(folded, f32),
             pltpu.VMEM((strip, QW), f32),
-            pltpu.VMEM((nb + 1, VEC_ROWS, D), f32),
-            pltpu.VMEM((nb + 1, VEC_ROWS, D), f32),
+            pltpu.VMEM((nb + 1, 8, D), f32),
+            pltpu.VMEM((nb + 1, 8, D), f32),
             pltpu.VMEM((nb + 2, *half), bf16),
             pltpu.VMEM((nb + 1, *half), bf16),
+            *[pltpu.VMEM((nb + 1, 16, D), f32)] * 2,
         ]
-        for plan, among in zip(plans, (widths, [QW])):
-            for m, first, size, order_of in plan:
-                scratch += Scatter.arrivals(nb, size, among[m])
-        scratch += dma(copies[0], copies[0], len(plans[0]), more, more, len(plans[1]))
+        for plan in plans:
+            for _, _, size, _ in plan:
+                scratch += Scatter.arrivals(nb, strip, size)
+        some = copies[0] + 2 * (nb + 1)
+        scratch += dma(some, some, len(plans[0]), more, more, len(plans[1]))
         grads = [v.reshape((2,) * (nb + 1) + (strip, v.shape[2])) for v in grads]
     else:
         grads = []
@@ -773,14 +809,15 @@
         grid=(nw, HEADS // GRP),
         in_specs=[
             kept((nw, WIN)), kept((2, 8, VW)), tok, tok, per((WIN, 3 * D)), EXPS, tok, tok, tok,
-            kept((D, 3 * D)), kept((D, D)), kept((8, D)), kept((8, D)), *[ANY] * len(grads),
+            kept((D, 3 * D)), kept((D, D)), kept((8, D)), kept((8, D)), kept((FLAT_PAD, WIDE_PAD)),
+            *[ANY] * len(grads),
         ],
         out_specs=out_specs,
         out_shape=out_shape,
         scratch_shapes=scratch,
         compiler_params=comm_params(3) if nb else PARAMS,
         name="attend_back",
-    )(order, vecs, xc, nrm, qkv, e, linv, att, mg, w, wo, feed, peak, *grads)
+    )(order, vecs, xc, nrm, qkv, e, linv, att, mg, w, wo, feed, peak, spread_constant(), *grads)
 
 
 BOTH = ("wide", "tensor")
@@ -793,7 +830,22 @@
 
 def orders_of(nb):
     down = tuple(reversed(range(nb)))
-    return (down, down[:-2] + (down[-1], down[-2])) if nb > 1 else (down, down)
+    if nb < 2:
+        return (down,)
+    half = nb // 2
+    swapped = down[:-2] + (down[-1], down[-2])
+    return (down, swapped, tuple(range(half)) + tuple(reversed(range(half, nb))))
+
+
+def cuts_of(width, count):
+    tiles = width // 128
+    sizes = [(tiles + count - 1 - i) // count for i in range(count)]
+    cuts, at = [], 0
+    for size in sizes:
+        if size:
+            cuts.append((at * 128, size * 128))
+            at += size
+    return cuts
 
 
 class Place:
@@ -832,14 +884,14 @@
         self.send, self.recv, self.near = send, recv, near
         nb = place.nb
         self.streams = []
+        orders = orders_of(nb)
         for own, buf in zip(owns, bufs):
-            strip = own.shape[0]
-            for half, order in enumerate(orders_of(nb)):
-                self.streams.append((own, buf, pl.ds(half * strip // 2, strip // 2), order))
+            for (first, size), order in zip(cuts_of(own.shape[1], len(orders)), orders):
+                self.streams.append((own, buf, first, size, order))
 
     @staticmethod
     def copies(nb, count):
-        return count * (2 * nb + 1)
+        return count * (len(orders_of(nb)) * nb + 1)
 
     def lanes(self, own):
         width = own.shape[1]
@@ -851,11 +903,12 @@
         return pltpu.make_async_copy(own, buf.at[(*mine, slice(None), self.lanes(own))], self.near.at[b])
 
     def wide(self, s, p):
-        own, buf, rows, order = self.streams[s]
+        own, buf, first, size, order = self.streams[s]
         place = self.place
         chosen = {k: place.bit[k] for k in order[p:]}
-        region = buf.at[(*place.index(chosen), rows, self.lanes(own))]
-        src = region if p else own.at[rows, :]
+        lanes = pl.ds(pl.multiple_of(place.t * own.shape[1] + first, 128), size)
+        region = buf.at[(*place.index(chosen), slice(None), lanes)]
+        src = region if p else own.at[:, pl.ds(first, size)]
         at = s * place.nb + p
         return remote(src, region, self.send.at[at], self.recv.at[at], place.across(order[p]))
 
@@ -905,7 +958,7 @@
 
     def local(self, s):
         matrix, first, size, order, (own, *arrive), out = self.streams[s]
-        src = matrix.at[(self.place.t, *self.place.index({}), pl.ds(first, size), slice(None))]
+        src = matrix.at[(self.place.t, *self.place.index({}), slice(None), pl.ds(first, size))]
         return pltpu.make_async_copy(src, own, self.near.at[s])
 
     def left(self, order, p):
@@ -915,7 +968,7 @@
         matrix, first, size, order, (own, *arrive), out = self.streams[s]
         place = self.place
         if p == 0:
-            src, to = matrix.at[(1 - place.t, *place.index({}), pl.ds(first, size), slice(None))], place.sibling()
+            src, to = matrix.at[(1 - place.t, *place.index({}), slice(None), pl.ds(first, size))], place.sibling()
         else:
             k = order[p - 1]
             src = arrive[p - 1].at[self.part(order, p, 1 - place.bit[k])]
@@ -944,7 +997,7 @@
             if left:
                 arrive[p][there] = total.astype(bf16)
             else:
-                out[first : first + size, :] = total
+                out[:, first : first + size] = total
             return carry
 
         if left:
@@ -973,13 +1026,14 @@
         return self.place.nb + 2
 
 
-GATHER_TIMES = (0.0, 0.07, 0.25, 0.44, 0.75, 0.94)
-SCATTER_TIMES = (0.0, 0.13, 0.5, 0.7, 0.88, 1.0)
-
-
-def run_beside(transfer, at_step, times):
+GATHER_TIMES = (0.0, 0.0, 0.0, 0.2, 0.5, 0.94)
+LATER_TIMES = (0.0, 0.2, 0.38, 0.57, 0.82, 0.94)
+SCATTER_TIMES = (0.0, 0.13, 0.44, 0.63, 0.82, 1.0)
+
+
+def run_beside(transfer, at_step, times, start=1):
     total = pl.num_programs(0) * pl.num_programs(1)
-    for p in range(1, transfer.steps()):
+    for p in range(start, transfer.steps()):
         when = times[min(p, len(times) - 1)]
         if when < 1.0:
 
@@ -994,12 +1048,12 @@
     )
 
 
-def stream_plan(nb, widths, strip):
-    first, second = (tuple(reversed(order)) for order in orders_of(nb))
+def stream_plan(nb, widths):
+    orders = [tuple(reversed(order)) for order in orders_of(nb)]
     plan = []
-    for m in range(len(widths)):
-        plan.append((m, 0, strip // 2, first))
-        plan.append((m, strip // 2, strip // 2, second))
+    for m, width in enumerate(widths):
+        for (first, size), order in zip(cuts_of(width, len(orders)), orders):
+            plan.append((m, first, size, order))
     return plan
 
 
@@ -1020,29 +1074,30 @@
         place = self.place
         to = place.across(p - 1) if p else place.sibling()
         at = self.base + 2 * p
+        vec = remote(self.vec.at[p], self.vec_in.at[p], self.send.at[at], self.recv.at[at], to)
+        if self.table is None:
+            return [vec]
         table = self.table.at[1 - place.t] if p == 0 else self.table.at[p + 1]
-        return (
-            remote(self.vec.at[p], self.vec_in.at[p], self.send.at[at], self.recv.at[at], to),
-            remote(table, self.table_in.at[p], self.send.at[at + 1], self.recv.at[at + 1], to),
-        )
-
-    def step(self, p, vec_out, table_out):
+        return [vec, remote(table, self.table_in.at[p], self.send.at[at + 1], self.recv.at[at + 1], to)]
+
+    def step(self, p, vec_out, table_out=None):
         nb = self.place.nb
         if p:
-            vec, table = self.pair(p - 1)
-            vec.wait_recv()
-            table.wait_recv()
+            for copy in self.pair(p - 1):
+                copy.wait_recv()
             mine, theirs = self.vec[p - 1], self.vec_in[p - 1]
-            summed = iota(mine.shape, 0) < SUM_ROWS
-            total = jnp.where(summed, mine + theirs, jnp.maximum(mine, theirs))
-            mine = self.table[self.place.t] if p == 1 else self.table[p]
-            table_total = mine.astype(f32) + self.table_in[p - 1].astype(f32)
+            total = jnp.where(iota(mine.shape, 0) < 8, mine + theirs, jnp.maximum(mine, theirs))
             if p <= nb:
                 self.vec[p] = total
-                self.table[p + 1] = table_total.astype(bf16)
             else:
                 vec_out[...] = total
-                table_out[...] = table_total
+            if self.table is not None:
+                mine = self.table[self.place.t] if p == 1 else self.table[p]
+                total = mine.astype(f32) + self.table_in[p - 1].astype(f32)
+                if p <= nb:
+                    self.table[p + 1] = total.astype(bf16)
+                else:
+                    table_out[...] = total
         if p <= nb:
             for copy in self.pair(p):
                 copy.start()
@@ -1079,7 +1134,7 @@
     if paired:
         first = jnp.concatenate([qv_bias[0], jnp.zeros((oc,), bf16), qv_bias[1], expand_bias])
         weights = [params(first), padded_table(rel_table), qkv_weight]
-        shards = [out_weight.T, expand_weight, reduce_weight.T]
+        shards = [expand_weight, reduce_weight.T, out_weight.T]
     else:
         qkv_strip = qkv_weight.reshape(strip, own, 3, HD).transpose(0, 2, 1, 3).reshape(strip, 3 * oc)
         shard = jnp.concatenate([qkv_strip, out_weight.T, expand_weight, reduce_weight.T], axis=1)
@@ -1105,16 +1160,15 @@
         nw, nb, order, region, inputs, weights, shards
     )
     if paired:
-        wo, we, wr = gathered
+        we, wr, wo = gathered
     layer_out, mg, gwe, gwr, gwo, feed = run_feed(nw, order, vecs, xc, att, cotangent, wo, we, wr)
-    input_grad, sums, table, qkv_own, *summed = run_back(
+    input_grad, late, table, *more = run_back(
         nw, nb, order, vecs, xc, nrm, qkv, e, linv, att, mg, wqkv, wo, feed, peak, [gwo, gwe, gwr]
     )
     if paired:
-        out_own, expand_own, reduce_own = summed
-        qkv_out = qkv_own
+        qkv_out, early, out_own, expand_own, reduce_own = more
     else:
-        gw = qkv_own
+        gw = more[0]
 
         def cut(grad, width):
             return grad.transpose(1, 0, 2).reshape(D, parts, width).astype(f32)
@@ -1129,16 +1183,15 @@
         out_own = grads[:, 3 * oc : 4 * oc]
         expand_own, reduce_own = grads[:, 4 * oc : 4 * oc + fc], grads[:, 4 * oc + fc :]
         table = lax.dynamic_slice_in_dim(lax.psum(table, BOTH), mine * own, own, 0)
-        sums = jnp.concatenate(
-            [lax.psum(sums[:SUM_ROWS], BOTH), lax.pmax(sums[SUM_ROWS:], BOTH)], axis=0
-        )
+        late = lax.psum(late, BOTH)
+        early = jnp.concatenate([lax.psum(feed, BOTH), lax.pmax(peak, BOTH)], axis=0)
 
     table_own = table[:, : 2 * WT - 1, :ROWS].reshape(own, RT)
-    dbe_own = lax.dynamic_slice_in_dim(sums[6:10].reshape(FF), mine * fc, fc, 0)
-    heads_grad = sums[10:13].reshape(2, 3, HALF)
+    dbe_own = lax.dynamic_slice_in_dim(early[4:8].reshape(FF), mine * fc, fc, 0)
+    heads_grad = late[2:5].reshape(2, 3, HALF)
     bias_grad = jnp.stack([heads_grad[:, 0].reshape(D), heads_grad[:, 2].reshape(D)], axis=0)
     bias_own = lax.dynamic_slice_in_dim(bias_grad, mine * oc, oc, 1)
-    peak_own = lax.dynamic_slice_in_dim(sums[SUM_ROWS], mine * own, own, 0)
+    peak_own = lax.dynamic_slice_in_dim(early[8], mine * own, own, 0)
     factor = jnp.sqrt(clip_threshold / jnp.maximum(peak_own, clip_threshold))
     column_factor = jnp.stack([factor, factor, jnp.ones_like(factor)], axis=1)
     clipped_qkv = (
@@ -1149,19 +1202,19 @@
     return (
         layer_out,
         input_grad,
-        sums[0],
-        sums[1],
+        late[0],
+        late[1],
         qkv_out,
         bias_own,
         table_own,
         out_own.T,
-        sums[5],
-        sums[2],
-        sums[3],
+        early[3],
+        early[0],
+        early[1],
         expand_own,
         dbe_own,
         reduce_own.T,
-        sums[4],
+        early[2],
         peak_own,
         clipped_qkv,
         clipped_bias,

time: 225 us -> 236 us (1.049); the launches traced: 224 us -> 232 us
  Pallas kernels: 199 us -> 207 us
    pallas_call x1, Pallas kernels: 85.8 us -> 101 us  [run_back(): pl.pallas_call(functools.partial(back_kernel, nb, plans), grid=(nw, HEADS...]
    pallas_call x1, Pallas kernels: 71.1 us -> 63.5 us  [run_attend(): pl.pallas_call(functools.partial(attend_kernel, nw, nb), grid=(nw, HEADS...]
where the time goes in v3:
time: 236 us; the launch traced here: 232 us
  Pallas kernels  207 us (88%)
  local copies, waits for them, and re-layouts  18.8 us (8%)
  other arithmetic  5.42 us (2%)
    pallas_call x1, Pallas kernels, run_back(): pl.pallas_call(functools.partial(back_kernel, nb, plans), grid=(nw, HEADS...  101 us
    pallas_call x1, Pallas kernels, run_attend(): pl.pallas_call(functools.partial(attend_kernel, nw, nb), grid=(nw, HEADS...  63.5 us
    pallas_call x1, Pallas kernels, run_feed(): pl.pallas_call(feed_kernel, grid=(nw,), in_specs=[kept((nw, WIN)), kept((...  42.2 us
    unnamed x21, local copies, waits for them, and re-layouts  6.71 us

profile of v3, /device:TPU:0, one launch (start us, length us, event | category | flops | bytes accessed | tf_op | source)
XLA Modules:
  0.0 232.4 jit_solution(15006729942012077101)
XLA Ops:
  0.7 0.0 copy-start
  0.7 0.7 copy-done
  1.4 0.6 constant_dynamic-slice_fusion.1.order_ref
  2.0 0.8 dynamic-slice_convert_fusion
  2.8 0.7 convert_element_type.20.region_ref
  3.4 0.8 slice_reduce_fusion.1
  4.2 0.7 pad_maximum_fusion
  4.9 0.7 stack.32
  5.6 0.7 stack.33
  6.3 0.7 stack.34
  7.0 0.7 stack.35
  7.7 0.7 stack.36
  8.3 0.7 stack.37
  9.1 0.6 fusion.2.rest_0_
  9.7 1.0 reshape.99
  10.7 0.7 pad_convert_fusion.rest_1_
  11.3 63.5 %attend.1 = (bf16[1568,512]{1,0:T(8,128)(2,1)}, bf16[1568,512]{1,0:T(8,128)(2,1)}, bf16[1568,1536]{1,0:T(8,128)(2,1)}, bf16[4,16,392,392]{3,2,1,0:T(8,128)(2,1)}...) custom-call(s32[4,392]{1,0:T(4,128)} %constant_dynamic-slice_fusion., ...), custom_call_target="tpu_custom_call" | custom-call | tf_op jit(solution)/shard_map/attend/pallas_call | solution.py:694
  74.8 42.2 %feed.1 = (bf16[1568,512]{1,0:T(8,128)(2,1)}, f32[1568,512]{1,0:T(8,128)}, bf16[2,512,1024]{2,1,0:T(8,128)(2,1)}, bf16[2,512,1024]{2,1,0:T(8,128)(2,1)}, bf16[2,512,256]{2,1,0:T(8,128)(2,1)}, /*index=5*/f32[8,512]{1,0:T(8,128)}) custom-call(s32[4,392]{1,0:T(4,128)} %constant_dynamic-slice_fusion.1.order_ref, f32[2,8,1792]{2,1,0:T(8,128)} %get-tuple-element.44.vecs_ref, ...), custom_call_target="tpu_custom_call" | custom-call | tf_op jit(solution)/shard_map/feed/pallas_call | solution.py:714
  117.0 0.0 copy-start.1
  117.0 0.0 copy-start.6
  117.0 100.8 %attend_back.1 = (bf16[1568,512]{1,0:T(8,128)(2,1)}, f32[8,512]{1,0:T(8,128)}, f32[8,16,256]{2,1,0:T(8,128)}, f32[32,768]{1,0:T(8,128)}, f32[16,512]{1,0:T(8,128...) custom-call(s32[4,392]{1,0:T(4,128)} %constant_dynamic-slice_fusion.1.order_ref, ...), custom_call_target="tpu_custom_call" | custom-call | tf_op jit(solution)/shard_map/attend_back/pallas_call | solution.py:807
  217.9 0.0 copy-start.4
  217.9 1.5 fusion.6
  220.1 0.1 sqrt_bitcast_fusion
  220.1 0.1 pad.16.clone
  220.2 0.1 maximum_maximum_fusion
  220.3 0.1 copy.38
  220.4 0.1 mul.37
  220.4 0.1 mul.38
  220.5 0.7 convert_multiply_fusion
  221.2 0.8 slice.46
  222.0 0.7 fusion.3
  222.6 0.6 divide_sqrt_fusion
  223.2 0.1 broadcast_in_dim.12
  223.3 0.1 stack_reshape.3
  223.4 0.0 copy-done.6
  223.4 0.6 pad_multiply_fusion
  224.0 1.7 reshape.107
  225.6 0.7 slice_bitcast_fusion
  226.3 0.6 dynamic_slice.20
  226.9 2.7 %copy.46 = bf16[1568,512]{1,0:T(8,128)(2,1)} copy(bf16[1568,512]{1,0:T(8,128)(2,1)} %get-tuple-element.104) | data formatting | bytes 3211264
  229.6 0.0 copy-done.4
  229.6 0.6 copy.47
  230.3 0.6 copy.48
  230.9 0.0 copy-done.3
  230.9 0.7 copy.49
  231.5 0.0 copy-done.2
  231.5 0.7 copy.50
  (12 shorter events, 0.1 us)
Async XLA Ops:
  0.7 0.7 copy-start
  117.0 103.5 %copy-start.1 = (bf16[32,768]{1,0:T(8,128)(2,1)S(1)}, bf16[32,768]{1,0:T(8,128)(2,1)}, u32[]{:S(2)}) copy-start(bf16[32,768]{1,0:T(8,128)(2,1)} %rest_2_.1) | copy-start | bytes 147460
  117.0 106.3 %copy-start.6 = (bf16[2,256]{1,0:T(2,128)(2,1)S(1)}, bf16[2,256]{1,0:T(2,128)(2,1)}, u32[]{:S(2)}) copy-start(bf16[2,256]{1,0:T(2,128)(2,1)} %param.27) | copy-start | bytes 3076
  217.9 11.7 %copy-start.4 = (f32[32,768]{1,0:T(8,128)S(1)}, f32[32,768]{1,0:T(8,128)}, u32[]{:S(2)}) copy-start(f32[32,768]{1,0:T(8,128)} %get-tuple-element.107) | copy-start | bytes 294916
  217.9 12.4 %copy-start.5 = (f32[32,256]{1,0:T(8,128)S(1)}, f32[32,256]{1,0:T(8,128)}, u32[]{:S(2)}) copy-start(f32[32,256]{1,0:T(8,128)} %get-tuple-element.66) | copy-start | bytes 98308
  217.9 13.0 %copy-start.3 = (f32[32,1024]{1,0:T(8,128)S(1)}, f32[32,1024]{1,0:T(8,128)}, u32[]{:S(2)}) copy-start(f32[32,1024]{1,0:T(8,128)} %get-tuple-element.114) | copy-start | bytes 393220
  221.2 10.3 %copy-start.2 = (f32[32,1024]{1,0:T(8,128)S(1)}, f32[32,1024]{1,0:T(8,128)}, u32[]{:S(2)}) copy-start(f32[32,1024]{1,0:T(8,128)} %get-tuple-element.69) | copy-start | bytes 393220

commit v4 on v2

--- a/solution.py
+++ b/solution.py
@@ -793,7 +793,22 @@
 
 def orders_of(nb):
     down = tuple(reversed(range(nb)))
-    return (down, down[:-2] + (down[-1], down[-2])) if nb > 1 else (down, down)
+    if nb < 2:
+        return (down,)
+    half = nb // 2
+    swapped = down[:-2] + (down[-1], down[-2])
+    return (down, swapped, tuple(range(half)) + tuple(reversed(range(half, nb))))
+
+
+def cuts_of(width, count):
+    tiles = width // 128
+    sizes = [(tiles + count - 1 - i) // count for i in range(count)]
+    cuts, at = [], 0
+    for size in sizes:
+        if size:
+            cuts.append((at * 128, size * 128))
+            at += size
+    return cuts
 
 
 class Place:
@@ -832,14 +847,14 @@
         self.send, self.recv, self.near = send, recv, near
         nb = place.nb
         self.streams = []
+        orders = orders_of(nb)
         for own, buf in zip(owns, bufs):
-            strip = own.shape[0]
-            for half, order in enumerate(orders_of(nb)):
-                self.streams.append((own, buf, pl.ds(half * strip // 2, strip // 2), order))
+            for (first, size), order in zip(cuts_of(own.shape[1], len(orders)), orders):
+                self.streams.append((own, buf, first, size, order))
 
     @staticmethod
     def copies(nb, count):
-        return count * (2 * nb + 1)
+        return count * (len(orders_of(nb)) * nb + 1)
 
     def lanes(self, own):
         width = own.shape[1]
@@ -851,11 +866,12 @@
         return pltpu.make_async_copy(own, buf.at[(*mine, slice(None), self.lanes(own))], self.near.at[b])
 
     def wide(self, s, p):
-        own, buf, rows, order = self.streams[s]
+        own, buf, first, size, order = self.streams[s]
         place = self.place
         chosen = {k: place.bit[k] for k in order[p:]}
-        region = buf.at[(*place.index(chosen), rows, self.lanes(own))]
-        src = region if p else own.at[rows, :]
+        lanes = pl.ds(pl.multiple_of(place.t * own.shape[1] + first, 128), size)
+        region = buf.at[(*place.index(chosen), slice(None), lanes)]
+        src = region if p else own.at[:, pl.ds(first, size)]
         at = s * place.nb + p
         return remote(src, region, self.send.at[at], self.recv.at[at], place.across(order[p]))
 
@@ -995,7 +1011,7 @@
 
 
 def stream_plan(nb, widths, strip):
-    first, second = (tuple(reversed(order)) for order in orders_of(nb))
+    first, second = (tuple(reversed(orders_of(nb)[i])) for i in (0, -1 if nb < 2 else 1))
     plan = []
     for m in range(len(widths)):
         plan.append((m, 0, strip // 2, first))

time: 225 us -> 222 us (0.987)
  Pallas kernels: 199 us -> 196 us
    pallas_call x1, Pallas kernels: 71.1 us -> 67.5 us  [run_attend(): pl.pallas_call(functools.partial(attend_kernel, nb), grid=(nw, HEADS // G...]
where the time goes in v4:
time: 222 us; the launch traced here: 221 us
  Pallas kernels  196 us (88%)
  local copies, waits for them, and re-layouts  19 us (9%)
  other arithmetic  4.84 us (2%)
    pallas_call x1, Pallas kernels, run_back(): pl.pallas_call(functools.partial(back_kernel, nb, plans), grid=(nw, HEADS...  86.4 us
    pallas_call x1, Pallas kernels, run_attend(): pl.pallas_call(functools.partial(attend_kernel, nb), grid=(nw, HEADS // G...  67.5 us
    pallas_call x1, Pallas kernels, run_feed(): pl.pallas_call(feed_kernel, grid=(nw,), in_specs=[kept((nw, WIN)), kept((...  42.1 us
    unnamed x21, local copies, waits for them, and re-layouts  6.8 us

profile of v4, /device:TPU:0, one launch (start us, length us, event | category | flops | bytes accessed | tf_op | source)
XLA Modules:
  0.0 221.2 jit_solution(3075917049558827827)
XLA Ops:
  0.7 0.0 copy-start
  0.7 0.7 copy-done
  1.4 0.6 constant_dynamic-slice_fusion.1.order_ref
  2.0 0.8 dynamic-slice_convert_fusion
  2.8 0.7 convert_element_type.20.region_ref
  3.4 0.8 slice_reduce_fusion.1
  4.2 0.7 pad_maximum_fusion
  4.9 0.7 stack.32
  5.6 0.7 stack.33
  6.3 0.7 stack.34
  7.0 0.7 stack.35
  7.7 0.7 stack.36
  8.3 0.7 stack.37
  9.1 0.6 fusion.2.rest_0_
  9.7 1.0 reshape.95
  10.7 0.7 pad_convert_fusion.rest_1_
  11.3 67.5 %attend.1 = (bf16[1568,512]{1,0:T(8,128)(2,1)}, bf16[1568,512]{1,0:T(8,128)(2,1)}, bf16[1568,1536]{1,0:T(8,128)(2,1)}, bf16[4,16,392,392]{3,2,1,0:T(8,128)(2,1)}...) custom-call(s32[4,392]{1,0:T(4,128)} %constant_dynamic-slice_fusion., ...), custom_call_target="tpu_custom_call" | custom-call | tf_op jit(solution)/shard_map/attend/pallas_call | solution.py:661
  78.8 42.1 %feed.1 = (bf16[1568,512]{1,0:T(8,128)(2,1)}, f32[1568,512]{1,0:T(8,128)}, bf16[2,512,1024]{2,1,0:T(8,128)(2,1)}, bf16[2,512,1024]{2,1,0:T(8,128)(2,1)}, bf16[2,512,256]{2,1,0:T(8,128)(2,1)}, /*index=5*/f32[8,512]{1,0:T(8,128)}) custom-call(s32[4,392]{1,0:T(4,128)} %constant_dynamic-slice_fusion.1.order_ref, f32[2,8,1792]{2,1,0:T(8,128)} %get-tuple-element.43.vecs_ref, ...), custom_call_target="tpu_custom_call" | custom-call | tf_op jit(solution)/shard_map/feed/pallas_call | solution.py:681
  121.0 0.0 copy-start.6
  121.0 0.0 copy-start.1
  121.0 86.4 %attend_back.1 = (bf16[1568,512]{1,0:T(8,128)(2,1)}, f32[24,512]{1,0:T(8,128)}, f32[8,16,256]{2,1,0:T(8,128)}, f32[32,768]{1,0:T(8,128)}, f32[32,256]{1,0:T(8,12...) custom-call(s32[4,392]{1,0:T(4,128)} %constant_dynamic-slice_fusion.1.order_ref, f32[2,8,1792]{2,1,0:T(8,128)} %get-tuple-element.43.vecs_ref, ...), custom_call_target="tpu_custom_call" | custom-call | tf_op jit(solution)/shard_map/attend_back/pallas_call | solution.py:771
  207.4 1.5 fusion.6
  209.5 0.6 divide_sqrt_fusion
  210.1 0.1 broadcast_in_dim.12
  210.2 0.1 stack_reshape.3
  210.3 0.7 slice.46
  211.0 0.0 copy-done.6
  211.0 0.7 fusion.3
  211.7 0.1 sqrt_bitcast_fusion
  211.8 0.1 pad.16.clone
  211.9 0.1 maximum_maximum_fusion
  211.9 0.1 copy.37
  212.0 0.1 mul.37
  212.1 0.1 mul.38
  212.2 0.0 copy-done.1
  212.2 0.7 convert_multiply_fusion
  212.8 1.7 reshape.103
  214.5 0.8 slice_bitcast_fusion
  215.3 0.6 dynamic_slice.20
  215.9 2.7 %copy.45 = bf16[1568,512]{1,0:T(8,128)(2,1)} copy(bf16[1568,512]{1,0:T(8,128)(2,1)} %get-tuple-element.102) | data formatting | bytes 3211264
  218.6 0.0 copy-done.4
  218.6 0.6 copy.46
  219.2 0.0 copy-done.5
  219.2 0.6 copy.47
  219.9 0.0 copy-done.3
  219.9 0.7 copy.48
  220.5 0.0 copy-done.2
  220.5 0.7 copy.49
  (11 shorter events, 0.1 us)
Async XLA Ops:
  0.7 0.7 copy-start
  121.0 90.1 %copy-start.6 = (bf16[2,256]{1,0:T(2,128)(2,1)S(1)}, bf16[2,256]{1,0:T(2,128)(2,1)}, u32[]{:S(2)}) copy-start(bf16[2,256]{1,0:T(2,128)(2,1)} %param.26) | copy-start | bytes 3076
  121.0 91.2 %copy-start.1 = (bf16[32,768]{1,0:T(8,128)(2,1)S(1)}, bf16[32,768]{1,0:T(8,128)(2,1)}, u32[]{:S(2)}) copy-start(bf16[32,768]{1,0:T(8,128)(2,1)} %rest_2_.1) | copy-start | bytes 147460
  215.9 2.7 %copy-start.4 = (f32[32,768]{1,0:T(8,128)S(1)}, f32[32,768]{1,0:T(8,128)}, u32[]{:S(2)}) copy-start(f32[32,768]{1,0:T(8,128)} %get-tuple-element.105) | copy-start | bytes 294916
  215.9 3.4 %copy-start.5 = (f32[32,256]{1,0:T(8,128)S(1)}, f32[32,256]{1,0:T(8,128)}, u32[]{:S(2)}) copy-start(f32[32,256]{1,0:T(8,128)} %get-tuple-element.65) | copy-start | bytes 98308
  215.9 4.0 %copy-start.3 = (f32[32,1024]{1,0:T(8,128)S(1)}, f32[32,1024]{1,0:T(8,128)}, u32[]{:S(2)}) copy-start(f32[32,1024]{1,0:T(8,128)} %get-tuple-element.112) | copy-start | bytes 393220
  215.9 4.7 %copy-start.2 = (f32[32,1024]{1,0:T(8,128)S(1)}, f32[32,1024]{1,0:T(8,128)}, u32[]{:S(2)}) copy-start(f32[32,1024]{1,0:T(8,128)} %get-tuple-element.67) | copy-start | bytes 393220

commit v5 on v4

--- a/solution.py
+++ b/solution.py
@@ -990,7 +990,7 @@
 
 
 GATHER_TIMES = (0.0, 0.07, 0.25, 0.44, 0.75, 0.94)
-SCATTER_TIMES = (0.0, 0.13, 0.5, 0.7, 0.88, 1.0)
+SCATTER_TIMES = (0.0, 0.13, 0.44, 0.63, 0.82, 1.0)
 
 
 def run_beside(transfer, at_step, times):

time: 222 us -> 222 us (level)
  no operation moved by 1% of the time
where the time goes in v5:
time: 222 us; the launch traced here: 221 us
  Pallas kernels  196 us (88%)
  local copies, waits for them, and re-layouts  19 us (9%)
  other arithmetic  4.84 us (2%)
    pallas_call x1, Pallas kernels, run_back(): pl.pallas_call(functools.partial(back_kernel, nb, plans), grid=(nw, HEADS...  86.5 us
    pallas_call x1, Pallas kernels, run_attend(): pl.pallas_call(functools.partial(attend_kernel, nb), grid=(nw, HEADS // G...  67.5 us
    pallas_call x1, Pallas kernels, run_feed(): pl.pallas_call(feed_kernel, grid=(nw,), in_specs=[kept((nw, WIN)), kept((...  42.1 us
    unnamed x21, local copies, waits for them, and re-layouts  6.8 us

profile of v5, /device:TPU:0, one launch (start us, length us, event | category | flops | bytes accessed | tf_op | source)
XLA Modules:
  0.0 221.3 jit_solution(1430557792164500102)
XLA Ops:
  0.7 0.0 copy-start
  0.7 0.7 copy-done
  1.4 0.6 constant_dynamic-slice_fusion.1.order_ref
  2.0 0.8 dynamic-slice_convert_fusion
  2.8 0.7 convert_element_type.20.region_ref
  3.4 0.8 slice_reduce_fusion.1
  4.2 0.7 pad_maximum_fusion
  4.9 0.7 stack.32
  5.6 0.7 stack.33
  6.3 0.7 stack.34
  7.0 0.7 stack.35
  7.7 0.7 stack.36
  8.3 0.7 stack.37
  9.1 0.6 fusion.2.rest_0_
  9.7 1.0 reshape.95
  10.7 0.7 pad_convert_fusion.rest_1_
  11.3 67.5 %attend.1 = (bf16[1568,512]{1,0:T(8,128)(2,1)}, bf16[1568,512]{1,0:T(8,128)(2,1)}, bf16[1568,1536]{1,0:T(8,128)(2,1)}, bf16[4,16,392,392]{3,2,1,0:T(8,128)(2,1)}...) custom-call(s32[4,392]{1,0:T(4,128)} %constant_dynamic-slice_fusion., ...), custom_call_target="tpu_custom_call" | custom-call | tf_op jit(solution)/shard_map/attend/pallas_call | solution.py:661
  78.8 42.1 %feed.1 = (bf16[1568,512]{1,0:T(8,128)(2,1)}, f32[1568,512]{1,0:T(8,128)}, bf16[2,512,1024]{2,1,0:T(8,128)(2,1)}, bf16[2,512,1024]{2,1,0:T(8,128)(2,1)}, bf16[2,512,256]{2,1,0:T(8,128)(2,1)}, /*index=5*/f32[8,512]{1,0:T(8,128)}) custom-call(s32[4,392]{1,0:T(4,128)} %constant_dynamic-slice_fusion.1.order_ref, f32[2,8,1792]{2,1,0:T(8,128)} %get-tuple-element.43.vecs_ref, ...), custom_call_target="tpu_custom_call" | custom-call | tf_op jit(solution)/shard_map/feed/pallas_call | solution.py:681
  121.0 0.0 copy-start.6
  121.0 0.0 copy-start.1
  121.0 86.5 %attend_back.1 = (bf16[1568,512]{1,0:T(8,128)(2,1)}, f32[24,512]{1,0:T(8,128)}, f32[8,16,256]{2,1,0:T(8,128)}, f32[32,768]{1,0:T(8,128)}, f32[32,256]{1,0:T(8,12...) custom-call(s32[4,392]{1,0:T(4,128)} %constant_dynamic-slice_fusion.1.order_ref, f32[2,8,1792]{2,1,0:T(8,128)} %get-tuple-element.43.vecs_ref, ...), custom_call_target="tpu_custom_call" | custom-call | tf_op jit(solution)/shard_map/attend_back/pallas_call | solution.py:771
  207.5 1.5 fusion.6
  209.7 0.6 divide_sqrt_fusion
  210.3 0.1 broadcast_in_dim.12
  210.3 0.1 stack_reshape.3
  210.4 0.7 slice.46
  211.2 0.0 copy-done.6
  211.2 0.7 fusion.3
  211.8 0.1 sqrt_bitcast_fusion
  211.9 0.1 pad.16.clone
  212.0 0.1 maximum_maximum_fusion
  212.1 0.1 copy.37
  212.1 0.1 mul.37
  212.2 0.1 mul.38
  212.3 0.0 copy-done.1
  212.3 0.7 convert_multiply_fusion
  213.0 1.7 reshape.103
  214.6 0.8 slice_bitcast_fusion
  215.4 0.6 dynamic_slice.20
  216.0 2.7 %copy.45 = bf16[1568,512]{1,0:T(8,128)(2,1)} copy(bf16[1568,512]{1,0:T(8,128)(2,1)} %get-tuple-element.102) | data formatting | bytes 3211264
  218.7 0.0 copy-done.4
  218.7 0.6 copy.46
  219.4 0.0 copy-done.5
  219.4 0.6 copy.47
  220.0 0.0 copy-done.3
  220.0 0.7 copy.48
  220.6 0.0 copy-done.2
  220.6 0.7 copy.49
  (11 shorter events, 0.1 us)
Async XLA Ops:
  0.7 0.7 copy-start
  121.0 90.2 %copy-start.6 = (bf16[2,256]{1,0:T(2,128)(2,1)S(1)}, bf16[2,256]{1,0:T(2,128)(2,1)}, u32[]{:S(2)}) copy-start(bf16[2,256]{1,0:T(2,128)(2,1)} %param.26) | copy-start | bytes 3076
  121.0 91.3 %copy-start.1 = (bf16[32,768]{1,0:T(8,128)(2,1)S(1)}, bf16[32,768]{1,0:T(8,128)(2,1)}, u32[]{:S(2)}) copy-start(bf16[32,768]{1,0:T(8,128)(2,1)} %rest_2_.1) | copy-start | bytes 147460
  216.0 2.7 %copy-start.4 = (f32[32,768]{1,0:T(8,128)S(1)}, f32[32,768]{1,0:T(8,128)}, u32[]{:S(2)}) copy-start(f32[32,768]{1,0:T(8,128)} %get-tuple-element.105) | copy-start | bytes 294916
  216.0 3.4 %copy-start.5 = (f32[32,256]{1,0:T(8,128)S(1)}, f32[32,256]{1,0:T(8,128)}, u32[]{:S(2)}) copy-start(f32[32,256]{1,0:T(8,128)} %get-tuple-element.65) | copy-start | bytes 98308
  216.0 4.0 %copy-start.3 = (f32[32,1024]{1,0:T(8,128)S(1)}, f32[32,1024]{1,0:T(8,128)}, u32[]{:S(2)}) copy-start(f32[32,1024]{1,0:T(8,128)} %get-tuple-element.112) | copy-start | bytes 393220
  216.0 4.7 %copy-start.2 = (f32[32,1024]{1,0:T(8,128)S(1)}, f32[32,1024]{1,0:T(8,128)}, u32[]{:S(2)}) copy-start(f32[32,1024]{1,0:T(8,128)} %get-tuple-element.67) | copy-start | bytes 393220
